TPU v7x, 256 devices: a whole 4x4x8 slice. The times are simulated.
256 devices in a mesh: seq: 32 (over y_hi, z, core), chan: 8 (over y_lo, x).
Axes of the slice: x: 4, y: 4 (y_hi: 2, y_lo: 2; y = y_hi * 2 + y_lo), z: 8, core: 2. Of those that a mesh axis runs over, the one named last changes fastest.
Arguments:
- streams: bfloat16 [3, 256, 524288], P(None, 'chan', 'seq'), may hold values from -6 to 6
- conv_weights: float32 [3, 256, 3], P(None, 'chan'), may hold values from -3.5 to 3.5
- skip: float32 [256], P('chan'), may hold values from 0.5 to 1.5
- filter_spec: bfloat16 [8, 32, 2, 1048576], P('chan', 'seq'), may hold values from -6 to 6
- residual: bfloat16 [256, 524288], P('chan', 'seq'), may hold values from -27 to 27
- gain: float32 [256], P('chan'), may hold values from 0.5 to 1.5
Outputs:
- hidden_out: bfloat16 [256, 524288], P('chan', 'seq')
- normed: bfloat16 [256, 524288], P('chan', 'seq')
All inputs are finite; a program needn't handle non-finite values.
Results may differ from a plain program's by a relative error of at most 0.015.
Values may be sent and summed in bfloat16 or wider, within the bound.
A program may use at most 128 MiB of HBM per device.

v0:
```python
import math

import jax
import jax.numpy as jnp
from jax import lax
from jax.sharding import PartitionSpec as P


def passed_along(value, axis, steps):
    count = lax.axis_size(axis)
    initial, last = (max(0, -steps), min(count, count - steps))
    return lax.ppermute(value, axis, [(source, source + steps) for source in range(initial, last)])


def contract(form, first_op, second_op):
    return jnp.einsum(form, first_op, second_op, precision=lax.Precision.HIGHEST)


def twiddles(count_rows, count_cols, length, orient):
    product_idx = (
        jnp.arange(count_rows, dtype=jnp.int32)[:, None]
        * jnp.arange(count_cols, dtype=jnp.int32)[None, :]
        % length
    )
    angles = product_idx.astype(jnp.float32) * (2.0 * math.pi / length)
    return (jnp.cos(angles), orient * jnp.sin(angles))


def section_table(count_out, count_in, length, orient):
    cos_tab, sin_tab = twiddles(count_out, count_in, length, orient)
    return jnp.stack([jnp.stack([cos_tab, -sin_tab]), jnp.stack([sin_tab, cos_tab])])


def rotate(pair, count_rows, count_cols, length, orient):
    cos_tab, sin_tab = twiddles(count_rows, count_cols, length, orient)
    real_part = pair[0] * cos_tab - pair[1] * sin_tab
    imag_part = pair[0] * sin_tab + pair[1] * cos_tab
    return jnp.stack([real_part, imag_part])


def forward_pass(pair):
    length = pair.shape[-1]
    if length <= 128:
        return contract("cdkn,d...n->c...k", section_table(length, length, length, -1.0), pair)
    remain = length // 128
    grid = pair.reshape(pair.shape[:-1] + (128, remain))
    section = contract("cdkn,d...nb->c...kb", section_table(128, 128, 128, -1.0), grid)
    return forward_pass(rotate(section, 128, remain, length, -1.0))


def forward_real(signal, fft_len):
    remain = fft_len // 128
    used = signal.shape[-1] // remain
    grid = signal.reshape(signal.shape[:-1] + (used, remain))
    cos_tab, sin_tab = twiddles(128, used, 128, -1.0)
    section = contract("ckn,...nb->c...kb", jnp.stack([cos_tab, sin_tab]), grid)
    return forward_pass(rotate(section, 128, remain, fft_len, -1.0))


def inverse_pass(pair, length):
    if length <= 128:
        return contract("cdtk,d...k->c...t", section_table(length, length, length, 1.0), pair)
    remain = length // 128
    inner = inverse_pass(pair, remain)
    rotated = rotate(inner, 128, remain, length, 1.0)
    section = contract("cdtk,d...kb->c...tb", section_table(128, 128, 128, 1.0), rotated)
    return section.reshape(section.shape[:-2] + (length,))


def inverse_real(pair, fft_len, seq_len):
    remain = fft_len // 128
    inner = inverse_pass(pair, remain)
    rotated = rotate(inner, 128, remain, fft_len, 1.0)
    used = seq_len // remain
    cos_tab, sin_tab = twiddles(used, 128, 128, 1.0)
    out = contract("dtk,d...kb->...tb", jnp.stack([cos_tab, -sin_tab]), rotated)
    return out.reshape(out.shape[:-2] + (seq_len,))


def scramble(spectrum, fft_len):
    factors = []
    length = fft_len
    while length > 128:
        factors.append(128)
        length = length // 128
    factors.append(length)
    shaped = spectrum.reshape((2,) + tuple(reversed(factors)))
    count = len(factors)
    return jnp.transpose(shaped, (0,) + tuple(range(count, 0, -1)))


def long_filter(signal, spectrum):
    seq_len = signal.shape[-1]
    fft_len = spectrum.shape[-1]
    fwd = forward_real(signal.astype(jnp.float32), fft_len)
    spec = scramble(spectrum, fft_len).astype(jnp.float32)
    prod_real = fwd[0] * spec[0] - fwd[1] * spec[1]
    prod_imag = fwd[0] * spec[1] + fwd[1] * spec[0]
    product = jnp.stack([prod_real, prod_imag])
    return inverse_real(product, fft_len, seq_len) / fft_len


def short_conv(values, weights, before):
    kernel_len = weights.shape[-1]
    span_len = values.shape[-1]
    joined = jnp.concatenate([before, values], axis=-1).astype(jnp.float32)
    running = jnp.zeros(values.shape, jnp.float32)
    for offset in range(kernel_len):
        begin_at = kernel_len - 1 - offset
        running = (
            running
            + weights[..., offset : offset + 1] * joined[..., begin_at : begin_at + span_len]
        )
    return running


def per_device(streams, conv_weights, skip, filter_spec, residual, gain):
    slab_len = streams.shape[2]
    local_channels = streams.shape[1]
    kernel_len = conv_weights.shape[2]
    seq_index = lax.axis_index("seq")
    first_rim = passed_along(streams[0, :, slab_len - (kernel_len - 1) :], "seq", 1)
    gate_out = short_conv(streams[0], conv_weights[0], first_rim).astype(jnp.bfloat16)
    raw_pair = lax.all_to_all(streams[1:], "seq", split_axis=1, concat_axis=2, tiled=True)
    own_weights = lax.dynamic_slice_in_dim(conv_weights[1:], seq_index, 1, 1)
    zero_rim = jnp.zeros((2, 1, kernel_len - 1), jnp.bfloat16)
    own_filtered = short_conv(raw_pair, own_weights, zero_rim)
    whole_row = (own_filtered[0] * own_filtered[1]).astype(jnp.bfloat16)
    own_skip = lax.dynamic_slice_in_dim(skip, seq_index, 1, 0)
    convolved = long_filter(whole_row, filter_spec[0, 0]) + own_skip[:, None] * whole_row.astype(
        jnp.float32
    )
    long_out = convolved.astype(jnp.bfloat16)
    returned = lax.all_to_all(long_out, "seq", split_axis=1, concat_axis=0, tiled=True)
    hidden_out = (
        residual.astype(jnp.float32) + gate_out.astype(jnp.float32) * returned.astype(jnp.float32)
    ).astype(jnp.bfloat16)
    hidden_f = hidden_out.astype(jnp.float32)
    local_sq = jnp.sum(hidden_f * hidden_f, axis=0)
    total_sq = lax.psum(local_sq, "chan")
    channel_count = local_channels * lax.axis_size("chan")
    mean_sq = total_sq / channel_count
    normed = (hidden_f * gain[:, None] * lax.rsqrt(mean_sq + 1e-06)[None, :]).astype(jnp.bfloat16)
    return (hidden_out, normed)


def solution(mesh):
    in_specs = (
        P(None, "chan", "seq"),
        P(None, "chan", None),
        P("chan"),
        P("chan", "seq", None, None),
        P("chan", "seq"),
        P("chan"),
    )
    out_specs = (P("chan", "seq"), P("chan", "seq"))
    return jax.shard_map(
        per_device, mesh=mesh, in_specs=in_specs, out_specs=out_specs, check_vma=False
    )
```

profile of v0, /device:TPU:32, one launch (start us, length us, event | category | flops | bytes accessed | tf_op | source)
XLA Modules:
  0.0 409.1 jit_solution(18007967382494021823)
XLA Ops:
  7.2 1.6 slice-done.2
  8.8 3.5 copy.90
  12.3 11.4 %all-to-all-start = ((bf16[2,32,16384]{2,0,1:T(2,128)(2,1)}), bf16[2,32,16384]{2,0,1:T(2,128)(2,1)S(1)}, u32[]{:S(2)}, u32[]{:S(2)}) async-start(bf16[2,32,16384]{2,0,1:T(2,128)(2,1)} %copy.90), calls=%async_computation | async-start | bytes 4194304 | tf_op jit(solution)/shard_map/all_to_all | solution.py:124
  23.6 0.8 slice.109
  25.1 2.0 collective-permute-start
  29.2 0.8 broadcast_multiply_fusion.2
  30.7 5.0 %convert_bitcast_fusion = f32[1,2,8192,128]{3,1,2,0:T(2,128)S(1)} fusion(bf16[1,1,2,1048576]{3,2,1,0:T(2,128)(2,1)} %param.9), kind=kLoop, calls=%fused_computation.22 | loop fusion | flops 2097152 | bytes 12582912
  35.7 3.8 copy.92
  39.5 8.8 %copy.69 = f32[2,64,128,128]{2,1,3,0:T(8,128)} copy(f32[2,64,128,128]{3,2,1,0:T(8,128)} %bitcast.167) | data formatting | bytes 16777216 | tf_op jit(solution)/shard_map/convert_element_type | solution.py:96
  51.8 1.3 slice_bitcast_fusion.2
  53.1 23.5 %all-to-all-done = bf16[2,32,16384]{2,0,1:T(2,128)(2,1)S(1)} async-done(((bf16[2,32,16384]{2,0,1:T(2,128)(2,1)}), bf16[2,32,16384]{2,0,1:T(2,128)(2,1)S(1)}, u32[]{:S(2)}, u32[]{:S(2)}) %all-to-all-start) | async-done | bytes 2097184 | tf_op jit(solution)/shard_map/all_to_all | solution.py:124
  76.6 2.8 pad_convert_fusion
  79.4 9.0 %fusion.17 = f32[2,1,524288]{2,0,1:T(2,128)S(1)} fusion(f32[2,1,524290]{2,0,1:T(2,128)S(1)} %pad_convert_fusion, f32[2]{0:T(128)S(1)} %copy-done.15, f32[2]{0:T(128)S(1)} %copy-done.14, f32[2]{0:T(128)S(1)} %copy-done.13), kind=kLoop, calls=%fused_computation.32 | loop fusion | flops 5242880 | bytes 16777240 | tf_op jit(solution)/shard_map/add | solution.py:111
  88.4 26.8 %multiply_reduce_fusion = (f32[524288]{0:T(1024)}, bf16[1,1,524288]{2,0,1:T(2,128)(2,1)S(1)}) fusion(f32[]{:T(128)} %bitcast.65, f32[2,1,524288]{2,0,1:T(2,128)S(1)} %fusion.17), kind=kLoop, calls=%fused_computation.75 | loop fusion | flops 2097152 | bytes 7340036 | tf_op jit(solution)/shard_map/mul | solution.py:130
  115.1 23.2 %reduce.3 = bf16[524288]{0:T(1024)(128)(2,1)} reduce(bf16[1,1,524288]{2,0,1:T(2,128)(2,1)S(1)} %get-tuple-element.8, bf16[]{:T(256)} %constant.124), dimensions={0,1}, to_apply=%convert_element_type.272.reduce_sub_computation | reduce | bytes 2097154 | tf_op jit(solution)/shard_map/convert_element_type | solution.py:128
  138.4 1.5 reshape.732
  139.9 4.3 %convolution_bitcast_fusion = f32[2,1,128,8192]{2,3,0,1:T(8,128)S(1)} fusion(bf16[64,8192,1]{1,0,2:T(8,128)(2,1)S(1)} %reshape.732, f32[1,128,64]{1,2,0:T(8,128)} %get-tuple-element.32, f32[1,128,64]{1,2,0:T(8,128)} %get-tuple-element.33), kind=kOutput, calls=%fused_computation | convolution fusion | flops 1610629120 | bytes 9502720 | tf_op jit(solution)/shard_map/ckn,...nb->c...kb/dot_general | solution.py:16
  144.2 18.7 %multiply_subtract_fusion.2 = (f32[1,1,128,8192]{2,3,0,1:T(8,128)}, f32[1,1,128,8192]{2,3,0,1:T(8,128)}) fusion(f32[2,1,128,8192]{2,3,0,1:T(8,128)S(1)} %convolution_bitcast_fusion), kind=kLoop, calls=%fused_computation.49 | loop fusion | flops 22020096 | bytes 16777216 | tf_op jit(solution)/shard_map/sub | solution.py:36
  162.9 5.4 %copy.66 = f32[1,1,128,128,64]{3,2,0,4,1:T(8,128)} copy(f32[1,1,128,128,64]{2,4,3,1,0:T(8,128)} %bitcast.169) | data formatting | bytes 8388608 | tf_op jit(solution)/shard_map/stack | solution.py:38
  168.3 5.4 %copy.65 = f32[1,1,128,128,64]{3,2,0,4,1:T(8,128)} copy(f32[1,1,128,128,64]{2,4,3,1,0:T(8,128)} %bitcast.168) | data formatting | bytes 8388608 | tf_op jit(solution)/shard_map/stack | solution.py:38
  173.7 9.5 %fusion.31 = f32[2,1,128,128,64]{3,2,0,4,1:T(8,128)S(1)} fusion(f32[1,1,128,128,64]{3,2,0,4,1:T(8,128)} %copy.66, f32[1,1,128,128,64]{3,2,0,4,1:T(8,128)} %copy.65, f32[1,2,128,128]{3,2,1,0:T(8,128)S(1)} %get-tuple-element.23, f32[1,2,128,128]{3,2,1,0:T(8,128)S(1)} %copy-done.2), kind=kOutput, calls=%fused_computation.56 | convolution fusion | flops 6444613632 | bytes 17039360 | tf_op jit(solution)/shard_map/cdkn,d...nb->c...kb/dot_general | solution.py:16
  183.2 2.0 multiply_subtract_fusion.1
  185.2 1.1 maximum_bitcast_fusion.2
  186.4 13.6 %fusion.24 = f32[2,1,128,128,64]{3,4,0,2,1:T(8,128)S(1)} fusion(f32[2,128,128,64,1]{2,1,0,3,4:T(8,128)S(1)} %maximum_bitcast_fusion.2, f32[1,2,64,64]{3,2,1,0:T(8,128)S(1)} %copy-done.6, f32[1,2,64,64]{3,2,1,0:T(8,128)S(1)} %copy-done.7), kind=kOutput, calls=%fused_computation.53 | convolution fusion | flops 3221241856 | bytes 16842752 | tf_op jit(solution)/shard_map/cdkn,d...n->c...k/dot_general | solution.py:16
  200.0 2.4 subtract_bitcast_fusion
  202.5 8.9 %fusion.27 = f32[128,128,2,64]{1,3,2,0:T(8,128)S(1)} fusion(f32[1,2,64,64]{3,2,1,0:T(8,128)S(1)} %copy-done.5, f32[1,2,64,64]{3,2,1,0:T(8,128)S(1)} %copy-done.4, f32[1,1,128,128,64]{3,4,2,1,0:T(8,128)S(1)} %get-tuple-element.10, f32[1,1,128,128,64]{3,4,2,1,0:T(8,128)S(1)} %get-tuple-element.9), kind=kOutput, calls=%fused_computation.54 | convolution fusion | flops 3223339008 | bytes 16842752 | tf_op jit(solution)/shard_map/cdtk,d...k->c...t/dot_general | solution.py:16
  211.4 5.0 %copy.105 = f32[128,128,2,64]{1,0,2,3:T(8,128)S(1)} copy(f32[128,128,2,64]{1,3,2,0:T(8,128)S(1)} %fusion.27) | data formatting | bytes 16777216 | tf_op jit(solution)/shard_map/cdtk,d...k->c...t/dot_general | solution.py:16
  216.4 2.0 multiply_subtract_fusion
  218.4 8.4 %fusion.30 = f32[2,1,128,128,64]{2,3,0,4,1:T(8,128)S(1)} fusion(f32[1,1,128,128,64]{3,2,0,4,1:T(8,128)S(1)} %get-tuple-element.12, f32[1,1,128,128,64]{3,2,0,4,1:T(8,128)S(1)} %get-tuple-element.11, f32[1,2,128,128]{3,2,1,0:T(8,128)S(1)} %get-tuple-element.22, f32[1,2,128,128]{3,2,1,0:T(8,128)S(1)} %get-tuple-element.21), kind=kOutput, calls=%fused_computation.55 | convolution fusion | flops 6444613632 | bytes 17039360 | tf_op jit(solution)/shard_map/cdtk,d...kb->c...tb/dot_general | solution.py:16
  226.8 1.1 fusion.115
  227.9 2.6 copy.73
  230.6 2.4 copy.72
  233.0 17.9 %fusion.19 = (f32[1,1,128,8192]{2,3,0,1:T(8,128)S(1)}, f32[1,1,128,8192]{2,3,0,1:T(8,128)S(1)}) fusion(f32[1,1,128,128,64]{2,4,3,1,0:T(8,128)S(1)} %copy.73, f32[1,1,128,128,64]{2,4,3,1,0:T(8,128)S(1)} %copy.72), kind=kLoop, calls=%fused_computation.38 | loop fusion | flops 20971520 | bytes 16777216 | tf_op jit(solution)/shard_map/sub | solution.py:36
  251.0 8.2 %fusion.1 = f32[1,64,8192]{2,1,0:T(8,128)S(1)} fusion(f32[1,1,128,8192]{2,3,0,1:T(8,128)S(1)} %get-tuple-element.16, f32[1,1,128,8192]{2,3,0,1:T(8,128)S(1)} %get-tuple-element.15, f32[1,64,128]{2,1,0:T(8,128)S(1)} %copy-done.8, f32[1,64,128]{2,1,0:T(8,128)S(1)} %copy-done.9), kind=kOutput, calls=%fused_computation.3 | convolution fusion | flops 1613250560 | bytes 10551296 | tf_op jit(solution)/shard_map/dtk,d...kb->...tb/dot_general | solution.py:16
  259.2 1.7 div.22
  260.9 3.2 mul.1023
  264.2 1.8 add_convert_fusion
  266.0 2.2 copy.106
  268.7 8.0 %reduce.11 = bf16[32,16384]{1,0:T(8,128)(2,1)} reduce(bf16[32,1,16384]{2,1,0:T(2,128)(2,1)S(1)} %bitcast.171, bf16[]{:T(256)} %broadcast.988), dimensions={1}, to_apply=%bitcast.162.reduce_sub_computation | reduce | bytes 2097154
  276.8 2.6 reshape.758
  279.4 4.4 %all-to-all-start.1 = ((bf16[32,2,8192]{2,1,0:T(2,128)(2,1)}), bf16[32,2,8192]{2,1,0:T(2,128)(2,1)}, u32[]{:S(2)}, u32[]{:S(2)}) async-start(bf16[32,2,8192]{2,1,0:T(2,128)(2,1)} %reshape.758), calls=%async_computation.1 | async-start | bytes 2097152 | tf_op jit(solution)/shard_map/all_to_all | solution.py:134
  284.9 28.6 %all-to-all-done.1 = bf16[32,2,8192]{2,1,0:T(2,128)(2,1)} async-done(((bf16[32,2,8192]{2,1,0:T(2,128)(2,1)}), bf16[32,2,8192]{2,1,0:T(2,128)(2,1)}, u32[]{:S(2)}, u32[]{:S(2)}) %all-to-all-start.1) | async-done | bytes 1048608 | tf_op jit(solution)/shard_map/all_to_all | solution.py:134
  313.5 5.9 %reshape.759 = bf16[32,1,16384]{2,1,0:T(2,128)(2,1)} reshape(bf16[32,2,8192]{2,1,0:T(2,128)(2,1)} %all-to-all-done.1) | data formatting | bytes 2097152
  319.4 3.7 bitcast_convert_fusion
  323.2 3.9 fusion.34
  327.1 72.8 %all-reduce.3.cloned.1.call-done = f32[16384]{0:T(1024)} async-done(((f32[16384]{0:T(1024)}), f32[16384]{0:T(1024)}) %all-reduce.3.cloned.1.call-update) | async-done | bytes 65552 | tf_op jit(solution)/shard_map/psum | solution.py:140
  399.9 0.9 add_rsqrt_fusion
  400.8 1.3 fusion.33
  (66 shorter events, 8.7 us)
Async XLA Ops:
  7.2 1.6 slice-start.2
  12.3 64.3 %all-to-all-start = ((bf16[2,32,16384]{2,0,1:T(2,128)(2,1)}), bf16[2,32,16384]{2,0,1:T(2,128)(2,1)S(1)}, u32[]{:S(2)}, u32[]{:S(2)}) async-start(bf16[2,32,16384]{2,0,1:T(2,128)(2,1)} %copy.90), calls=%async_computation | async-start | bytes 4194304 | tf_op jit(solution)/shard_map/all_to_all | solution.py:124
  25.1 258.8 %collective-permute-start = (bf16[32,2]{0,1:T(2,128)(2,1)}, bf16[32,2]{0,1:T(2,128)(2,1)}, u32[]{:S(2)}, u32[]{:S(2)}) collective-permute-start(bf16[32,2]{0,1:T(2,128)(2,1)} %bitcast.2), channel_id=1, source_target_pairs={{0,8},{8,16},{16,24},{24,32},{32,40},{40,48},{48,56},{56,64},{64,7... | collective-permute-start | bytes 392 | tf_op jit(solution)/shard_map/ppermute | solution.py:12
  39.5 8.8 %copy-start.17 = (f32[32]{0:T(128)S(1)}, f32[32]{0:T(128)}, u32[]{:S(2)}) copy-start(f32[32]{0:T(128)} %param.8) | copy-start | bytes 388
  39.5 9.3 %slice-start.3 = ((f32[3,32,3]{1,2,0:T(4,128)}), f32[2,32,3]{1,2,0:T(4,128)S(1)}, s32[]{:S(2)}) async-start(f32[3,32,3]{1,2,0:T(4,128)} %param.7), calls=%async_computation.6 | async-start | bytes 8192 | tf_op jit(solution)/shard_map/slice | solution.py:125
  39.5 12.3 %copy-start.12 = (f32[3,32,3]{1,2,0:T(4,128)S(1)}, f32[3,32,3]{1,2,0:T(4,128)}, u32[]{:S(2)}) copy-start(f32[3,32,3]{1,2,0:T(4,128)} %param.7) | copy-start | bytes 3460
  51.8 27.6 %copy-start.13 = (f32[2]{0:T(128)S(1)}, f32[2]{0:T(128)}, u32[]{:S(2)}) copy-start(f32[2]{0:T(128)} %get-tuple-element.2) | copy-start | bytes 28
  51.8 27.6 %copy-start.14 = (f32[2]{0:T(128)S(1)}, f32[2]{0:T(128)}, u32[]{:S(2)}) copy-start(f32[2]{0:T(128)} %get-tuple-element.3) | copy-start | bytes 28
  51.8 27.6 %copy-start.15 = (f32[2]{0:T(128)S(1)}, f32[2]{0:T(128)}, u32[]{:S(2)}) copy-start(f32[2]{0:T(128)} %get-tuple-element.4) | copy-start | bytes 28
  168.3 5.4 %copy-start.2 = (f32[1,2,128,128]{3,2,1,0:T(8,128)S(1)}, f32[1,2,128,128]{3,2,1,0:T(8,128)}, u32[]{:S(2)}) copy-start(f32[1,2,128,128]{3,2,1,0:T(8,128)} %get-tuple-element.24) | copy-start | bytes 393220
  173.7 9.5 %copy-start.3 = (f32[128,64]{0,1:T(8,128)S(1)}, f32[128,64]{0,1:T(8,128)}, u32[]{:S(2)}) copy-start(f32[128,64]{0,1:T(8,128)} %get-tuple-element.39) | copy-start | bytes 98308
  173.7 9.5 %copy-start.10 = (f32[128,64]{0,1:T(8,128)S(1)}, f32[128,64]{0,1:T(8,128)}, u32[]{:S(2)}) copy-start(f32[128,64]{0,1:T(8,128)} %get-tuple-element.38) | copy-start | bytes 98308
  185.2 1.1 copy-start.6
  185.2 1.1 copy-start.7
  185.2 14.7 %slice-start = ((s8[8388608]{0:T(1024)(128)(4,1)}), s8[4194304]{0:T(1024)(128)(4,1)S(1)}, s32[]{:S(2)}) async-start(s8[8388608]{0:T(1024)(128)(4,1)} %bitcast.163), calls=%async_computation.3 | async-start | bytes 8388608
  186.4 13.6 %slice-start.1 = ((s8[8388608]{0:T(1024)(128)(4,1)}), s8[4194304]{0:T(1024)(128)(4,1)S(1)}, s32[]{:S(2)}) async-start(s8[8388608]{0:T(1024)(128)(4,1)} %bitcast.163), calls=%async_computation.4 | async-start | bytes 8388608
  200.0 2.5 copy-start.4
  200.0 2.5 copy-start.5
  211.3 5.0 %copy-start.11 = (f32[128,64]{0,1:T(8,128)S(1)}, f32[128,64]{0,1:T(8,128)}, u32[]{:S(2)}) copy-start(f32[128,64]{0,1:T(8,128)} %fusion.103) | copy-start | bytes 98308
  233.0 18.0 %copy-start.8 = (f32[1,64,128]{2,1,0:T(8,128)S(1)}, f32[1,64,128]{2,1,0:T(8,128)}, u32[]{:S(2)}) copy-start(f32[1,64,128]{2,1,0:T(8,128)} %get-tuple-element.44) | copy-start | bytes 98308
  233.0 18.0 %copy-start.9 = (f32[1,64,128]{2,1,0:T(8,128)S(1)}, f32[1,64,128]{2,1,0:T(8,128)}, u32[]{:S(2)}) copy-start(f32[1,64,128]{2,1,0:T(8,128)} %get-tuple-element.45) | copy-start | bytes 98308
  260.9 3.3 copy-start
  279.4 34.1 %all-to-all-start.1 = ((bf16[32,2,8192]{2,1,0:T(2,128)(2,1)}), bf16[32,2,8192]{2,1,0:T(2,128)(2,1)}, u32[]{:S(2)}, u32[]{:S(2)}) async-start(bf16[32,2,8192]{2,1,0:T(2,128)(2,1)} %reshape.758), calls=%async_computation.1 | async-start | bytes 2097152 | tf_op jit(solution)/shard_map/all_to_all | solution.py:134
  283.8 116.1 %all-reduce.3.cloned.1.call-start = ((), (), s32[]{:S(2)}) async-start(), calls=%async_computation.2 | async-start | bytes 131072 | tf_op jit(solution)/shard_map/psum | solution.py:140
  323.2 77.6 %copy-start.16 = (f32[32]{0:T(128)S(1)}, f32[32]{0:T(128)}, u32[]{:S(2)}) copy-start(f32[32]{0:T(128)} %param.11) | copy-start | bytes 388
  327.1 75.0 %copy-start.1 = (bf16[32,16384]{1,0:T(8,128)(2,1)}, bf16[32,16384]{1,0:T(8,128)(2,1)S(1)}, u32[]{:S(2)}) copy-start(bf16[32,16384]{1,0:T(8,128)(2,1)S(1)} %get-tuple-element.6) | copy-start | bytes 3145732
Sparse Core Ops, SparseCore 0:
  327.2 72.6 all-reduce.2
where the time goes:
time: 414 us; the launch traced here: 409 us
  other arithmetic  136 us (33%)
  waiting for transfers between devices  125 us (30%)
  local copies, waits for them, and re-layouts  62.2 us (15%)
  matrix products  52.8 us (13%)
  starting transfers between devices  17.9 us (4%)
  between operations  14.7 us (4%)
    psum x1, waiting for transfers between devices, per_device(): total_sq = lax.psum(local_sq, 'chan')  72.8 us
    dot_general x6, matrix products, contract(): jnp.einsum(form, first_op, second_op, precision=lax.Precision.HIGHEST)  52.8 us
    sub x4, other arithmetic, rotate(): real_part = pair[0] * cos_tab - pair[1] * sin_tab  40.6 us
    all_to_all x1, waiting for transfers between devices, per_device(): lax.all_to_all(long_out, 'seq', split_axis=1, concat_axis=0, tiled=True)  28.6 us
    mul x1, other arithmetic, per_device(): own_skip[:, None] * whole_row.astype(jnp.float32)  26.8 us
    all_to_all x1, waiting for transfers between devices, per_device(): lax.all_to_all(streams[1:], 'seq', split_axis=1, concat_axis=2, tiled=True)  23.5 us
    convert_element_type x1, other arithmetic, per_device(): whole_row = (own_filtered[0] * own_filtered[1]).astype(jnp.bfloat16)  23.2 us
    unnamed x45, local copies, waits for them, and re-layouts  16.4 us
  transfers between devices with their start and end apart: 4, of which 3 were waited for; matrix products, arithmetic and copies ran while one was open for 56% of the time, Pallas kernels for 0%

commit v1 on v0

v1 whole, which is shorter than its diff:
```python
import math
import numpy as np
import jax
import jax.numpy as jnp
from jax import lax
from jax.experimental import pallas as pl
from jax.experimental.pallas import tpu as pltpu
import ml_dtypes
from jax.sharding import PartitionSpec as P

F32 = jnp.float32
BF16 = jnp.bfloat16
ROWS = 33
SLOTS = 40


def make_tables():
    d = np.arange(128)
    ang = -2.0 * np.pi * ((d[:, None] * d[None, :]) % 128) / 128
    fr, fi = np.cos(ang), np.sin(ang)
    u = np.block([[fr, -fi], [fi, fr]])
    tables = np.stack([u, u.T]).astype(ml_dtypes.bfloat16)
    ang = -2.0 * np.pi * (d[:, None] * d[None, :]) / 16384
    t0 = np.stack([np.cos(ang), np.sin(ang)]).astype(np.float32)
    place = np.arange(16384).reshape(128, 128)
    ang = -2.0 * np.pi * (np.arange(ROWS)[:, None, None] * place[None]) / 1048576
    w1 = np.stack([np.cos(ang), np.sin(ang)], axis=1).astype(np.float32)
    pick = np.zeros((2, 2, SLOTS, 128))
    perm = np.zeros((2, 2, 64, 2, 2, 128))
    for lo in range(2):
        for k1 in range(ROWS):
            alone = k1 in (0, 32)
            pick[0, lo, k1, lo * 64 + k1] = 2.0 ** -20 if alone else 2.0 ** -21
            if not alone:
                pick[1, lo, k1, lo * 64 + 64 - k1] = 2.0 ** -21
        for hi in range(64):
            k2 = 2 * hi + lo
            for part in range(2):
                perm[0, lo, hi, part, part, k2] = 1.0
                perm[1, lo, hi, part, part, 127 - k2] = 1.0 - 2.0 * part
    pick = pick.reshape(4 * SLOTS, 128).astype(ml_dtypes.bfloat16)
    perm = perm.reshape(512, 256).astype(ml_dtypes.bfloat16)
    return tables, t0, w1, pick, perm


def times(a, b, conj=False):
    if conj:
        return (a[0] * b[0] + a[1] * b[1], a[1] * b[0] - a[0] * b[1])
    return (a[0] * b[0] - a[1] * b[1], a[0] * b[1] + a[1] * b[0])


def turn(z, k, n, orient):
    re, im = z
    if k == 0:
        return z
    if 4 * k == n:
        if im is None:
            return (None, re if orient > 0 else -re)
        return (-im, re) if orient > 0 else (im, -re)
    c = math.cos(2.0 * math.pi * k / n)
    s = orient * math.sin(2.0 * math.pi * k / n)
    if im is None:
        return (re * c, re * s)
    if 8 * k == n:
        if orient > 0:
            return ((re - im) * c, (re + im) * c)
        return ((re + im) * c, (im - re) * c)
    return (re * c - im * s, re * s + im * c)


def plus(a, b):
    if a is None:
        return b
    if b is None:
        return a
    return a + b


def minus(a, b):
    if b is None:
        return a
    if a is None:
        return -b
    return a - b


def real_forward(vals, n):
    if n == 2:
        return [(vals[0], None), (vals[0], None)]
    even = real_forward(vals[0::2], n // 2)
    odd = real_forward(vals[1::2], n // 2)
    out = [None] * (n // 2 + 1)
    for k in range(n // 4 + 1):
        t = turn(odd[k], k, n, -1)
        e = even[k]
        out[k] = (plus(e[0], t[0]), plus(e[1], t[1]))
        if n // 2 - k != k:
            out[n // 2 - k] = (minus(e[0], t[0]), minus(t[1], e[1]))
    return out


def real_inverse(bins, n):
    if n == 2:
        return [bins[0][0] + bins[1][0]]
    even, odd = [], []
    for k in range(n // 4 + 1):
        a, b = bins[k], bins[n // 2 - k]
        even.append((plus(a[0], b[0]), minus(a[1], b[1])))
        t = (minus(a[0], b[0]), plus(a[1], b[1]))
        if k == n // 4:
            even[-1] = (a[0] + a[0], None)
            t = (None, a[1] + a[1])
            odd.append(turn_imag(t[1]))
        else:
            odd.append(turn(t, k, n, 1))
    first = real_inverse(even, n // 2)
    second = real_inverse(odd, n // 2)
    out = [None] * (n // 2)
    out[0::2] = first
    out[1::2] = second
    return out


def turn_imag(im):
    return (-im, None)


def filter_step(pairs_at, h_at, sh, pick, perm, direct):
    pieces = []
    for a, b in pairs_at:
        got = {}
        for name, k3 in (("a", a), ("b", b)):
            got[name] = lax.dot_general(
                pick, h_at(k3), (((1,), (1,)), ((), ())), preferred_element_type=F32
            ).astype(BF16)
        for mine, other in (("a", "b"), ("b", "a")):
            own, mirror = got[mine], got[other]
            pieces.append(
                jnp.concatenate(
                    [
                        own[0:SLOTS],
                        own[SLOTS : 2 * SLOTS],
                        mirror[2 * SLOTS : 3 * SLOTS],
                        mirror[3 * SLOTS : 4 * SLOTS],
                    ],
                    axis=1,
                )
            )
    joined = jnp.concatenate(pieces, axis=0)
    z = jnp.dot(joined, perm, preferred_element_type=F32)
    i = 0
    for a, b in pairs_at:
        for k3 in (a, b):
            zz = z[i * SLOTS : (i + 1) * SLOTS]
            sh[pl.ds(k3, SLOTS, stride=256), :] = zz[:, :128] + direct
            sh[pl.ds(128 + k3, SLOTS, stride=256), :] = zz[:, 128:]
            i += 1


def filter_prep(h_ref, sh, hs, pick_ref, perm_ref, direct, unroll=4):
    pick = pick_ref[...]
    perm = perm_ref[...]

    def h_at(k3):
        return h_ref[pl.ds(pl.multiple_of(k3 * 128, 128), 128), :]

    def step(i, c):
        filter_step(
            [(i * unroll + j, 127 - (i * unroll + j)) for j in range(unroll)],
            h_at, sh, pick, perm, direct,
        )
        return c

    lax.fori_loop(0, 64 // unroll, step, 0)

    def turn_over(i, c):
        for part in range(2):
            row = pl.multiple_of(i * 256 + part * 128, 128)
            hs[i, part] = sh[pl.ds(row, 128), :].T
        return c

    lax.fori_loop(0, ROWS, turn_over, 0)


def stage_one(load, a_ref, w1_ref, row, height=16):
    bins = real_forward([load(s) for s in range(32)], 64)
    for k1 in range(ROWS):
        re, im = bins[k1]
        if k1 == 0:
            im = jnp.zeros_like(re)
        else:
            wr = w1_ref[k1, 0, pl.ds(row, height), :]
            wi = w1_ref[k1, 1, pl.ds(row, height), :]
            if im is None:
                re, im = re * wr, re * wi
            else:
                re, im = times((re, im), (wr, wi))
        a_ref[k1, pl.ds(row, height), :] = re.astype(BF16)
        a_ref[k1, pl.ds(128 + row, height), :] = im.astype(BF16)


def middle(rows, a_ref, g_ref, hs, u, v, t0_ref):
    tr, ti = t0_ref[0], t0_ref[1]
    packed = jnp.concatenate([a_ref[k] for k in rows], axis=1)
    b = jnp.dot(u, packed, preferred_element_type=F32)
    lines = []
    for i, k in enumerate(rows):
        br, bi = b[:128, i * 128 : (i + 1) * 128], b[128:, i * 128 : (i + 1) * 128]
        re, im = times((br, bi), (tr, ti))
        lines.append(jnp.concatenate([re.astype(BF16), im.astype(BF16)], axis=1))
    c = jnp.dot(jnp.concatenate(lines, axis=0), v, preferred_element_type=F32)
    lines = []
    for i, k in enumerate(rows):
        cc = c[i * 128 : (i + 1) * 128]
        re, im = times((cc[:, :128], cc[:, 128:]), (hs[k, 0], hs[k, 1]))
        lines.append(jnp.concatenate([re.astype(BF16), im.astype(BF16)], axis=1))
    e = jnp.dot(jnp.concatenate(lines, axis=0), u, preferred_element_type=F32)
    cols = []
    for i, k in enumerate(rows):
        ee = e[i * 128 : (i + 1) * 128]
        re, im = times((ee[:, :128], ee[:, 128:]), (tr, ti), conj=True)
        cols.append(jnp.concatenate([re.astype(BF16), im.astype(BF16)], axis=0))
    g = jnp.dot(v, jnp.concatenate(cols, axis=1), preferred_element_type=F32)
    for i, k in enumerate(rows):
        g_ref[k] = g[:, i * 128 : (i + 1) * 128]


def all_middle(a_ref, g_ref, hs, uv_ref, t0_ref):
    u, v = uv_ref[0], uv_ref[1]

    def step(i, c):
        middle([2 * i, 2 * i + 1], a_ref, g_ref, hs, u, v, t0_ref)
        return c

    lax.fori_loop(0, 16, step, 0, unroll=4)
    middle([32], a_ref, g_ref, hs, u, v, t0_ref)


def stage_last(g_ref, w1_ref, row, height=16):
    bins = []
    for k1 in range(ROWS):
        re = g_ref[k1, pl.ds(row, height), :]
        im = g_ref[k1, pl.ds(128 + row, height), :]
        if k1 == 0:
            bins.append((re, None))
            continue
        wr = w1_ref[k1, 0, pl.ds(row, height), :]
        wi = w1_ref[k1, 1, pl.ds(row, height), :]
        if k1 == 32:
            bins.append((re * wr + im * wi, None))
        else:
            bins.append(times((re, im), (wr, wi), conj=True))
    return real_inverse(bins, 64)


SEQ = 32
CHAN = 8
SLAB = 16384
CHUNKS = 4
PC = 128 // CHUNKS
LANES = PC * 128
TILES = 4
MESH = pl.DeviceIdType.MESH


def hop(i):
    return lax.rem(i * 11, SEQ)


def fused(
    streams, wts, skip, h2, residual, gain, uv_in, t0_in, w1_in, pick_in, perm_in,
    out_h, out_n,
    st, flat, sb, xb, hv, sh, hs, a, g, uv, t0, w1, pick, perm, yb, rb,
    gate, res, hb, nb, sqp, sqa, rs, wb,
    load_sem, halo_sem, x_send, x_recv, y_send, y_recv, s_send, s_recv, o_sem,
):
    me = lax.axis_index("seq")
    mc = lax.axis_index("chan")

    loads = [
        pltpu.make_async_copy(
            streams.at[pl.ds(1, 2)], st.at[pl.ds(1, 2), :, pl.ds(128, SLAB)], load_sem.at[0]
        ),
        pltpu.make_async_copy(h2, hv, load_sem.at[1]),
        pltpu.make_async_copy(pick_in, pick, load_sem.at[2]),
        pltpu.make_async_copy(perm_in, perm, load_sem.at[3]),
        pltpu.make_async_copy(
            streams.at[pl.ds(0, 1)], st.at[pl.ds(0, 1), :, pl.ds(128, SLAB)], load_sem.at[4]
        ),
        pltpu.make_async_copy(w1_in, w1, load_sem.at[5]),
        pltpu.make_async_copy(uv_in, uv, load_sem.at[6]),
        pltpu.make_async_copy(t0_in, t0, load_sem.at[7]),
        pltpu.make_async_copy(residual, res, load_sem.at[8]),
    ]
    for copy in loads:
        copy.start()

    barrier = pltpu.get_barrier_semaphore()

    def greet_seq(i, c):
        pl.semaphore_signal(
            barrier, inc=1, device_id={"seq": lax.rem(me + i, SEQ)}, device_id_type=MESH
        )
        return c

    def greet_chan(i, c):
        pl.semaphore_signal(
            barrier, inc=1, device_id={"chan": lax.rem(mc + i, CHAN)}, device_id_type=MESH
        )
        return c

    lax.fori_loop(1, SEQ, greet_seq, 0)
    lax.fori_loop(1, CHAN, greet_chan, 0)

    eye = lax.broadcasted_iota(jnp.int32, (32, 32), 0) == lax.broadcasted_iota(
        jnp.int32, (32, 32), 1
    )

    def spread(row):
        column = jnp.sum(jnp.where(eye, row, 0.0), axis=1, keepdims=True)
        return jnp.broadcast_to(column, (32, 128))

    for stream in range(3):
        for tap in range(3):
            wb[stream * 3 + tap] = spread(wts[stream, pl.ds(tap, 1), :])
    wb[9] = spread(gain[...])

    pl.semaphore_wait(barrier, SEQ + CHAN - 2)

    halo = pltpu.make_async_remote_copy(
        src_ref=streams.at[:, :, pl.ds(SLAB - 128, 128)],
        dst_ref=st.at[:, :, pl.ds(0, 128)],
        send_sem=halo_sem.at[0],
        recv_sem=halo_sem.at[1],
        device_id={"seq": lax.rem(me + 1, SEQ)},
        device_id_type=MESH,
    )
    halo.start()

    lane = lax.broadcasted_iota(jnp.int32, (32, 128), 1)

    def short_conv(stream, first):
        cur = [
            st[stream, :, pl.ds(pl.multiple_of((first + i) * 128, 128), 128)].astype(F32)
            for i in range(TILES + 1)
        ]
        one = [pltpu.roll(t, 1, 1) for t in cur]
        two = [pltpu.roll(t, 2, 1) for t in cur]
        out = []
        for i in range(1, TILES + 1):
            back1 = jnp.where(lane < 1, one[i - 1], one[i])
            back2 = jnp.where(lane < 2, two[i - 1], two[i])
            out.append(
                wb[stream * 3] * cur[i] + wb[stream * 3 + 1] * back1 + wb[stream * 3 + 2] * back2
            )
        return out

    def gate_in(i, c):
        first = i * TILES
        one, two = short_conv(1, first), short_conv(2, first)
        for k in range(TILES):
            flat[pl.ds(pl.multiple_of((first + k) * 32, 32), 32), :] = one[k] * two[k]
        return c

    def send_chunk(j):
        lax.fori_loop(j * (PC // TILES), (j + 1) * (PC // TILES), gate_in, 0)

        def one_row(c):
            return flat[pl.ds(j * (PC * 32) + c, PC, stride=32), :].astype(BF16)

        rows = pl.ds(pl.multiple_of(j * PC, PC), PC)

        def send(i, c):
            peer = lax.rem(me + hop(i), SEQ)
            sb[peer, rows, :] = one_row(peer)
            pltpu.make_async_remote_copy(
                src_ref=sb.at[peer, rows],
                dst_ref=xb.at[j, me],
                send_sem=x_send.at[j],
                recv_sem=x_recv.at[j],
                device_id={"seq": peer},
                device_id_type=MESH,
            ).start()
            return c

        lax.fori_loop(1, SEQ, send, 0)
        xb[j, me] = one_row(me)

    loads[0].wait()

    def send_later(i, c):
        send_chunk(i + 1)
        return c

    lax.fori_loop(0, CHUNKS - 1, send_later, 0)
    loads[4].wait()
    halo.wait()
    st[:, :, pl.ds(0, 128)] = jnp.where(me > 0, st[:, :, pl.ds(0, 128)], jnp.zeros((3, 32, 128), BF16))
    send_chunk(0)

    for i in (1, 2, 3):
        loads[i].wait()
    filter_prep(hv, sh, hs, pick, perm, skip[me] * 2.0**-20)

    def gate_tiles(i, c):
        first = i * TILES
        vals = short_conv(0, first)
        for k in range(TILES):
            gate[:, pl.ds(pl.multiple_of((first + k) * 128, 128), 128)] = vals[k].astype(BF16)
        return c

    lax.fori_loop(0, 128 // TILES, gate_tiles, 0)
    for i in (5, 6, 7, 8):
        loads[i].wait()

    def all_of(buf, j, sem):
        return pltpu.make_async_copy(
            buf.at[j, pl.ds(0, SEQ - 1)], buf.at[j, pl.ds(0, SEQ - 1)], sem.at[j]
        )

    def first_stage(i, c):
        j = lax.rem(i + 1, CHUNKS)
        all_of(xb, j, x_recv).wait()

        def part(k, c):
            r = pl.multiple_of(k * 16, 16)
            stage_one(
                lambda s: xb[j, s, pl.ds(r, 16), :].astype(F32),
                a, w1, pl.multiple_of(j * PC + k * 16, 16),
            )
            return c

        lax.fori_loop(0, PC // 16, part, 0)
        return c

    lax.fori_loop(0, CHUNKS, first_stage, 0)
    all_middle(a, g, hs, uv, t0)

    def last_stage(j, c):
        def part(k, c):
            ys = stage_last(g, w1, pl.multiple_of(j * PC + k * 16, 16))
            for s in range(SEQ):
                yb[j, s, pl.ds(pl.multiple_of(k * 16, 16), 16), :] = ys[s].astype(BF16)
            return c

        lax.fori_loop(0, PC // 16, part, 0)

        def send(i, c):
            peer = lax.rem(me + hop(i), SEQ)
            pltpu.make_async_remote_copy(
                src_ref=yb.at[j, peer],
                dst_ref=rb.at[j, me],
                send_sem=y_send.at[j],
                recv_sem=y_recv.at[j],
                device_id={"seq": peer},
                device_id_type=MESH,
            ).start()
            return c

        lax.fori_loop(1, SEQ, send, 0)
        rb[j, me] = yb[j, me]
        return c

    lax.fori_loop(0, CHUNKS, last_stage, 0)

    def combine(j, c):
        all_of(rb, j, y_recv).wait()

        def spread_row(ch, c):
            flat[pl.ds(j * (PC * 32) + ch, PC, stride=32), :] = rb[j, ch].astype(F32)
            return c

        lax.fori_loop(0, 32, spread_row, 0, unroll=4)

        def tile(r, c):
            p = j * PC + r
            cols = pl.ds(pl.multiple_of(p * 128, 128), 128)
            long_out = flat[pl.ds(pl.multiple_of(p * 32, 32), 32), :]
            hidden = (res[:, cols].astype(F32) + gate[:, cols].astype(F32) * long_out).astype(BF16)
            hb[:, cols] = hidden
            wide = hidden.astype(F32)
            sqp[j, pl.ds(r, 1), :] = jnp.sum(wide * wide, axis=0, keepdims=True)
            return c

        lax.fori_loop(0, PC, tile, 0, unroll=4)

        def send(i, c):
            pltpu.make_async_remote_copy(
                src_ref=sqp.at[j],
                dst_ref=sqa.at[j, mc],
                send_sem=s_send.at[j],
                recv_sem=s_recv.at[j],
                device_id={"chan": lax.rem(mc + i, CHAN)},
                device_id_type=MESH,
            ).start()
            return c

        lax.fori_loop(1, CHAN, send, 0)
        sqa[j, mc] = sqp[j]
        cols = pl.ds(pl.multiple_of(j * LANES, LANES), LANES)
        pltpu.make_async_copy(hb.at[:, cols], out_h.at[:, cols], o_sem.at[0, j]).start()
        return c

    def norm(j, c):
        pltpu.make_async_copy(
            sqa.at[j, pl.ds(0, CHAN - 1)], sqa.at[j, pl.ds(0, CHAN - 1)], s_recv.at[j]
        ).wait()
        total = sqa[j, 0]
        for k in range(1, CHAN):
            total = total + sqa[j, k]
        rs[...] = lax.rsqrt(total * (1.0 / (32 * CHAN)) + 1e-06)

        def tile(r, c):
            cols = pl.ds(pl.multiple_of((j * PC + r) * 128, 128), 128)
            scale = wb[9] * rs[pl.ds(r, 1), :]
            nb[:, cols] = (hb[:, cols].astype(F32) * scale).astype(BF16)
            return c

        lax.fori_loop(0, PC, tile, 0, unroll=4)
        cols = pl.ds(pl.multiple_of(j * LANES, LANES), LANES)
        pltpu.make_async_copy(nb.at[:, cols], out_n.at[:, cols], o_sem.at[1, j]).start()
        return c

    combine(0, 0)

    def both(j, c):
        combine(j, c)
        return norm(j - 1, c)

    lax.fori_loop(1, CHUNKS, both, 0)
    norm(CHUNKS - 1, 0)

    def finish(j, c):
        all_of(xb, j, x_send).wait()
        all_of(rb, j, y_send).wait()
        pltpu.make_async_copy(
            sqa.at[j, pl.ds(0, CHAN - 1)], sqa.at[j, pl.ds(0, CHAN - 1)], s_send.at[j]
        ).wait()
        cols = pl.ds(pl.multiple_of(j * LANES, LANES), LANES)
        pltpu.make_async_copy(hb.at[:, cols], out_h.at[:, cols], o_sem.at[0, j]).wait()
        pltpu.make_async_copy(nb.at[:, cols], out_n.at[:, cols], o_sem.at[1, j]).wait()
        return c

    lax.fori_loop(0, CHUNKS, finish, 0)


def per_device(streams, conv_weights, skip, filter_spec, residual, gain):
    tables = [jnp.asarray(t) for t in make_tables()]
    h2 = filter_spec.reshape(2, 8192, 128).transpose(1, 0, 2).reshape(16384, 128)
    far = pl.BlockSpec(memory_space=pl.ANY)
    near = pl.BlockSpec(memory_space=pltpu.VMEM)
    slab = (32, SLAB)
    dma = pltpu.SemaphoreType.DMA
    vmem = pltpu.VMEM
    return pl.pallas_call(
        fused,
        out_shape=[jax.ShapeDtypeStruct(slab, BF16)] * 2,
        in_specs=[far, near, pl.BlockSpec(memory_space=pltpu.SMEM), far, far, near] + [far] * 5,
        out_specs=[far, far],
        scratch_shapes=[
            vmem((3, 32, 128 + SLAB), BF16),
            vmem((4096, 128), F32),
            vmem((32, 128, 128), BF16),
            vmem((CHUNKS, 32, PC, 128), BF16),
            vmem((16384, 128), BF16),
            vmem((SLOTS * 256, 128), F32),
            vmem((ROWS, 2, 128, 128), F32),
            vmem((ROWS, 256, 128), BF16),
            vmem((ROWS, 256, 128), F32),
            vmem((2, 256, 256), BF16),
            vmem((2, 128, 128), F32),
            vmem((ROWS, 2, 128, 128), F32),
            vmem((4 * SLOTS, 128), BF16),
            vmem((512, 256), BF16),
            vmem((CHUNKS, 32, PC, 128), BF16),
            vmem((CHUNKS, 32, PC, 128), BF16),
            vmem(slab, BF16),
            vmem(slab, BF16),
            vmem(slab, BF16),
            vmem(slab, BF16),
            vmem((CHUNKS, PC, 128), F32),
            vmem((CHUNKS, CHAN, PC, 128), F32),
            vmem((PC, 128), F32),
            vmem((10, 32, 128), F32),
            dma((9,)),
            dma((2,)),
            dma((CHUNKS,)),
            dma((CHUNKS,)),
            dma((CHUNKS,)),
            dma((CHUNKS,)),
            dma((CHUNKS,)),
            dma((CHUNKS,)),
            dma((2, CHUNKS)),
        ],
        compiler_params=pltpu.CompilerParams(
            collective_id=0, has_side_effects=True, vmem_limit_bytes=60 * 2**20
        ),
        cost_estimate=pl.CostEstimate(
            flops=8 * 10**9, bytes_accessed=20 * 2**20, transcendentals=0
        ),
    )(
        streams,
        conv_weights.transpose(0, 2, 1),
        skip,
        h2,
        residual,
        gain.reshape(1, 32),
        *tables,
    )


def solution(mesh):
    in_specs = (
        P(None, "chan", "seq"),
        P(None, "chan", None),
        P("chan"),
        P("chan", "seq", None, None),
        P("chan", "seq"),
        P("chan"),
    )
    out_specs = [P("chan", "seq"), P("chan", "seq")]
    return jax.shard_map(
        lambda *args: tuple(per_device(*args)),
        mesh=mesh,
        in_specs=in_specs,
        out_specs=tuple(out_specs),
        check_vma=False,
    )
```

time: 414 us -> 87.5 us (0.21)
  the two profiles are of different devices: /device:TPU:32 before, /device:TPU:1 now
where the time goes in v1:
time: 87.5 us; the launch traced here: 87.3 us
  Pallas kernels  82.2 us (94%)
  local copies, waits for them, and re-layouts  4.52 us (5%)
    pallas_call x1, Pallas kernels, per_device(): pl.pallas_call(fused, out_shape=[jax.ShapeDtypeStruct(slab, BF16)] * 2, i...  82.2 us
    unnamed x2, local copies, waits for them, and re-layouts  4.52 us

profile of v1, /device:TPU:1, one launch (start us, length us, event | category | flops | bytes accessed | tf_op | source)
XLA Modules:
  0.0 87.3 jit_solution(14724502549715520490)
XLA Ops:
  0.6 82.2 %shard_map.122 = (bf16[32,16384]{1,0:T(8,128)(2,1)}, bf16[32,16384]{1,0:T(8,128)(2,1)}) custom-call(bf16[3,32,16384]{2,1,0:T(8,128)(2,1)} %streams.1, f32[3,3,32]{2,1,0:T(4,128)} %bitcast.8, f32[32]{0:T(128)} %skip.1, bf16[16384,128]{1,0:T(8,128)(2,1)} %bitcast.7, bf16[32,16384]{1,0:T(8,128)(2,1)} %residual.1, f32[1,32]{1,0:T(1,128)} %bitcast.9, ...), custom_call_target="tpu_custom_call" | custom-call | flops 8000000000 | bytes 20971520 | tf_op jit(solution)/shard_map/pallas_call | solution.py:555
  82.8 2.3 %copy.16 = bf16[32,16384]{1,0:T(8,128)(2,1)} copy(bf16[32,16384]{1,0:T(8,128)(2,1)} %get-tuple-element.4) | data formatting | bytes 2097152
  85.1 2.3 %copy.17 = bf16[32,16384]{1,0:T(8,128)(2,1)} copy(bf16[32,16384]{1,0:T(8,128)(2,1)} %get-tuple-element.5) | data formatting | bytes 2097152

commit v2 on v1

v2 whole, which is shorter than its diff:
```python
import math
import numpy as np
import jax
import jax.numpy as jnp
from jax import lax
from jax.experimental import pallas as pl
from jax.experimental.pallas import tpu as pltpu
import ml_dtypes
from jax.sharding import PartitionSpec as P

F32 = jnp.float32
BF16 = jnp.bfloat16
ROWS = 33
SLOTS = 40


def make_tables():
    d = np.arange(128)
    ang = -2.0 * np.pi * ((d[:, None] * d[None, :]) % 128) / 128
    fr, fi = np.cos(ang), np.sin(ang)
    u = np.block([[fr, -fi], [fi, fr]])
    tables = np.stack([u, u.T]).astype(ml_dtypes.bfloat16)
    ang = -2.0 * np.pi * (d[:, None] * d[None, :]) / 16384
    t0 = np.stack([np.cos(ang), np.sin(ang)]).astype(np.float32)
    place = np.arange(16384).reshape(128, 128)
    ang = -2.0 * np.pi * (np.arange(ROWS)[:, None, None] * place[None]) / 1048576
    w1 = np.stack([np.cos(ang), np.sin(ang)], axis=1).astype(np.float32)
    pick = np.zeros((2, 2, SLOTS, 128))
    perm = np.zeros((2, 2, 64, 2, 2, 128))
    for lo in range(2):
        for k1 in range(ROWS):
            alone = k1 in (0, 32)
            pick[0, lo, k1, lo * 64 + k1] = 2.0 ** -20 if alone else 2.0 ** -21
            if not alone:
                pick[1, lo, k1, lo * 64 + 64 - k1] = 2.0 ** -21
        for hi in range(64):
            k2 = 2 * hi + lo
            for part in range(2):
                perm[0, lo, hi, part, part, k2] = 1.0
                perm[1, lo, hi, part, part, 127 - k2] = 1.0 - 2.0 * part
    pick = pick.reshape(4 * SLOTS, 128).astype(ml_dtypes.bfloat16)
    perm = perm.reshape(512, 256).astype(ml_dtypes.bfloat16)
    return tables, t0, w1, pick, perm


def times(a, b, conj=False):
    if conj:
        return (a[0] * b[0] + a[1] * b[1], a[1] * b[0] - a[0] * b[1])
    return (a[0] * b[0] - a[1] * b[1], a[0] * b[1] + a[1] * b[0])


def turn(z, k, n, orient):
    re, im = z
    if k == 0:
        return z
    if 4 * k == n:
        if im is None:
            return (None, re if orient > 0 else -re)
        return (-im, re) if orient > 0 else (im, -re)
    c = math.cos(2.0 * math.pi * k / n)
    s = orient * math.sin(2.0 * math.pi * k / n)
    if im is None:
        return (re * c, re * s)
    if 8 * k == n:
        if orient > 0:
            return ((re - im) * c, (re + im) * c)
        return ((re + im) * c, (im - re) * c)
    return (re * c - im * s, re * s + im * c)


def plus(a, b):
    if a is None:
        return b
    if b is None:
        return a
    return a + b


def minus(a, b):
    if b is None:
        return a
    if a is None:
        return -b
    return a - b


def real_forward(vals, n):
    if n == 2:
        return [(vals[0], None), (vals[0], None)]
    even = real_forward(vals[0::2], n // 2)
    odd = real_forward(vals[1::2], n // 2)
    out = [None] * (n // 2 + 1)
    for k in range(n // 4 + 1):
        t = turn(odd[k], k, n, -1)
        e = even[k]
        out[k] = (plus(e[0], t[0]), plus(e[1], t[1]))
        if n // 2 - k != k:
            out[n // 2 - k] = (minus(e[0], t[0]), minus(t[1], e[1]))
    return out


def real_inverse(bins, n):
    if n == 2:
        return [bins[0][0] + bins[1][0]]
    even, odd = [], []
    for k in range(n // 4 + 1):
        a, b = bins[k], bins[n // 2 - k]
        even.append((plus(a[0], b[0]), minus(a[1], b[1])))
        t = (minus(a[0], b[0]), plus(a[1], b[1]))
        if k == n // 4:
            even[-1] = (a[0] + a[0], None)
            t = (None, a[1] + a[1])
            odd.append(turn_imag(t[1]))
        else:
            odd.append(turn(t, k, n, 1))
    first = real_inverse(even, n // 2)
    second = real_inverse(odd, n // 2)
    out = [None] * (n // 2)
    out[0::2] = first
    out[1::2] = second
    return out


def turn_imag(im):
    return (-im, None)


def filter_step(pairs_at, h_at, sh, pick, perm, direct):
    pieces = []
    for a, b in pairs_at:
        got = {}
        for name, k3 in (("a", a), ("b", b)):
            got[name] = lax.dot_general(
                pick, h_at(k3), (((1,), (1,)), ((), ())), preferred_element_type=F32
            ).astype(BF16)
        for mine, other in (("a", "b"), ("b", "a")):
            own, mirror = got[mine], got[other]
            pieces.append(
                jnp.concatenate(
                    [
                        own[0:SLOTS],
                        own[SLOTS : 2 * SLOTS],
                        mirror[2 * SLOTS : 3 * SLOTS],
                        mirror[3 * SLOTS : 4 * SLOTS],
                    ],
                    axis=1,
                )
            )
    joined = jnp.concatenate(pieces, axis=0)
    z = jnp.dot(joined, perm, preferred_element_type=F32)
    i = 0
    for a, b in pairs_at:
        for k3 in (a, b):
            zz = z[i * SLOTS : (i + 1) * SLOTS]
            sh[pl.ds(k3, SLOTS, stride=256), :] = zz[:, :128] + direct
            sh[pl.ds(128 + k3, SLOTS, stride=256), :] = zz[:, 128:]
            i += 1


def filter_prep(h_ref, sh, hs, pick_ref, perm_ref, direct, unroll=4):
    pick = pick_ref[...]
    perm = perm_ref[...]

    def h_at(k3):
        return h_ref[pl.ds(pl.multiple_of(k3 * 128, 128), 128), :]

    def step(i, c):
        filter_step(
            [(i * unroll + j, 127 - (i * unroll + j)) for j in range(unroll)],
            h_at, sh, pick, perm, direct,
        )
        return c

    lax.fori_loop(0, 64 // unroll, step, 0)

    def turn_over(i, c):
        for part in range(2):
            row = pl.multiple_of(i * 256 + part * 128, 128)
            hs[i, part] = sh[pl.ds(row, 128), :].T
        return c

    lax.fori_loop(0, ROWS, turn_over, 0)


def stage_one(load, a_ref, w1_ref, row, height=16):
    bins = real_forward([load(s) for s in range(32)], 64)
    for k1 in range(ROWS):
        re, im = bins[k1]
        if k1 == 0:
            im = jnp.zeros_like(re)
        else:
            wr = w1_ref[k1, 0, pl.ds(row, height), :]
            wi = w1_ref[k1, 1, pl.ds(row, height), :]
            if im is None:
                re, im = re * wr, re * wi
            else:
                re, im = times((re, im), (wr, wi))
        a_ref[k1, pl.ds(row, height), :] = re.astype(BF16)
        a_ref[k1, pl.ds(128 + row, height), :] = im.astype(BF16)


def middle(groups, a_ref, g_ref, hs, u, v, t0_ref):
    tr, ti = t0_ref[0], t0_ref[1]

    def along_lanes(re, im):
        return jnp.concatenate([re.astype(BF16), im.astype(BF16)], axis=1)

    b = [
        jnp.dot(
            u, jnp.concatenate([a_ref[k] for k in rows], axis=1), preferred_element_type=F32
        )
        for rows in groups
    ]
    lines = []
    for rows, x in zip(groups, b):
        lines.append(
            jnp.concatenate(
                [
                    along_lanes(
                        *times(
                            (x[:128, i * 128 : (i + 1) * 128], x[128:, i * 128 : (i + 1) * 128]),
                            (tr, ti),
                        )
                    )
                    for i in range(len(rows))
                ],
                axis=0,
            )
        )
    c = [jnp.dot(x, v, preferred_element_type=F32) for x in lines]
    lines = []
    for rows, x in zip(groups, c):
        lines.append(
            jnp.concatenate(
                [
                    along_lanes(
                        *times(
                            (x[i * 128 : (i + 1) * 128, :128], x[i * 128 : (i + 1) * 128, 128:]),
                            (hs[k, 0], hs[k, 1]),
                        )
                    )
                    for i, k in enumerate(rows)
                ],
                axis=0,
            )
        )
    e = [jnp.dot(x, u, preferred_element_type=F32) for x in lines]
    lines = []
    for rows, x in zip(groups, e):
        cols = []
        for i in range(len(rows)):
            re, im = times(
                (x[i * 128 : (i + 1) * 128, :128], x[i * 128 : (i + 1) * 128, 128:]),
                (tr, ti),
                conj=True,
            )
            cols.append(jnp.concatenate([re.astype(BF16), im.astype(BF16)], axis=0))
        lines.append(jnp.concatenate(cols, axis=1))
    g = [jnp.dot(v, x, preferred_element_type=F32) for x in lines]
    for rows, x in zip(groups, g):
        for i, k in enumerate(rows):
            g_ref[k] = x[:, i * 128 : (i + 1) * 128]


def all_middle(a_ref, g_ref, hs, uv_ref, t0_ref):
    u, v = uv_ref[0], uv_ref[1]
    pairs = [[2 * i, 2 * i + 1] for i in range(16)]
    middle(pairs[:8], a_ref, g_ref, hs, u, v, t0_ref)
    middle(pairs[8:] + [[32]], a_ref, g_ref, hs, u, v, t0_ref)


def stage_last(g_ref, w1_ref, row, height=16):
    bins = []
    for k1 in range(ROWS):
        re = g_ref[k1, pl.ds(row, height), :]
        im = g_ref[k1, pl.ds(128 + row, height), :]
        if k1 == 0:
            bins.append((re, None))
            continue
        wr = w1_ref[k1, 0, pl.ds(row, height), :]
        wi = w1_ref[k1, 1, pl.ds(row, height), :]
        if k1 == 32:
            bins.append((re * wr + im * wi, None))
        else:
            bins.append(times((re, im), (wr, wi), conj=True))
    return real_inverse(bins, 64)


SEQ = 32
CHAN = 8
SLAB = 16384
TILES = 4
MESH = pl.DeviceIdType.MESH
THERE = [(0, 32, 32), (1, 64, 32), (2, 96, 32), (3, 16, 16), (4, 0, 16)]
BACK = [(0, 0, 16), (1, 16, 32), (2, 48, 32), (3, 80, 32), (4, 112, 16)]


def each_peer(fn, count, per):
    def step(i, c):
        for k in range(per):
            fn(i * per + k + 1)
        return c

    whole = (count - 1) // per
    lax.fori_loop(0, whole, step, 0)
    for i in range(whole * per + 1, count):
        fn(i)


def fused(
    streams, wts, skip, h2, residual, gain, uv_in, t0_in, w1_in, pick_in, perm_in,
    out_h, out_r,
    st, flat, sb, xb, hv, sh, hs, a, g, uv, t0, w1, pick, perm, yb, rb,
    gate, res, hb, sqp, sqa, rs, wb,
    load_sem, halo_sem, x_send, x_recv, y_send, y_recv, s_send, s_recv, o_sem,
):
    me = lax.axis_index("seq")
    mc = lax.axis_index("chan")

    def seq_peer(i):
        return lax.rem(me + i * 11, SEQ)

    def chan_peer(i):
        return lax.rem(mc + i, CHAN)

    loads = [
        pltpu.make_async_copy(
            streams.at[pl.ds(1, 2)], st.at[pl.ds(1, 2), :, pl.ds(128, SLAB)], load_sem.at[0]
        ),
        pltpu.make_async_copy(h2, hv, load_sem.at[1]),
        pltpu.make_async_copy(pick_in, pick, load_sem.at[2]),
        pltpu.make_async_copy(perm_in, perm, load_sem.at[3]),
        pltpu.make_async_copy(
            streams.at[pl.ds(0, 1)], st.at[pl.ds(0, 1), :, pl.ds(128, SLAB)], load_sem.at[4]
        ),
        pltpu.make_async_copy(w1_in, w1, load_sem.at[5]),
        pltpu.make_async_copy(uv_in, uv, load_sem.at[6]),
        pltpu.make_async_copy(t0_in, t0, load_sem.at[7]),
        pltpu.make_async_copy(residual, res, load_sem.at[8]),
    ]
    loads[0].start()

    barrier = pltpu.get_barrier_semaphore()

    def greet_seq(i):
        pl.semaphore_signal(
            barrier, inc=1, device_id={"seq": lax.rem(me + i, SEQ)}, device_id_type=MESH
        )

    def greet_chan(i):
        pl.semaphore_signal(barrier, inc=1, device_id={"chan": chan_peer(i)}, device_id_type=MESH)

    each_peer(greet_seq, SEQ, 5)
    each_peer(greet_chan, CHAN, 7)

    eye = lax.broadcasted_iota(jnp.int32, (32, 32), 0) == lax.broadcasted_iota(
        jnp.int32, (32, 32), 1
    )

    def spread(row):
        column = jnp.sum(jnp.where(eye, row, 0.0), axis=1, keepdims=True)
        return jnp.broadcast_to(column, (32, 128))

    for stream in range(3):
        for tap in range(3):
            wb[stream * 3 + tap] = spread(wts[stream, pl.ds(tap, 1), :])

    lane = lax.broadcasted_iota(jnp.int32, (32, 128), 1)

    def short_conv(stream, first):
        cur = [
            st[stream, :, pl.ds(pl.multiple_of((first + i) * 128, 128), 128)].astype(F32)
            for i in range(TILES + 1)
        ]
        one = [pltpu.roll(t, 1, 1) for t in cur]
        two = [pltpu.roll(t, 2, 1) for t in cur]
        out = []
        for i in range(1, TILES + 1):
            back1 = jnp.where(lane < 1, one[i - 1], one[i])
            back2 = jnp.where(lane < 2, two[i - 1], two[i])
            out.append(
                wb[stream * 3] * cur[i] + wb[stream * 3 + 1] * back1 + wb[stream * 3 + 2] * back2
            )
        return out

    def gate_rows(start, rows):
        def gate_in(i, c):
            first = start + i * TILES
            one, two = short_conv(1, first), short_conv(2, first)
            for k in range(TILES):
                flat[pl.ds(pl.multiple_of((first + k) * 32, 32), 32), :] = one[k] * two[k]
            return c

        lax.fori_loop(0, rows // TILES, gate_in, 0)

    def one_row(start, rows, c):
        return flat[pl.ds(start * 32 + c, rows, stride=32), :].astype(BF16)

    def send_rows(n, start, rows):
        span = pl.ds(pl.multiple_of(start, 16), rows)

        def send(i):
            peer = seq_peer(i)
            sb[peer, span, :] = one_row(start, rows, peer)
            pltpu.make_async_remote_copy(
                src_ref=sb.at[peer, span],
                dst_ref=xb.at[me, span],
                send_sem=x_send.at[n],
                recv_sem=x_recv.at[n],
                device_id={"seq": peer},
                device_id_type=MESH,
            ).start()

        each_peer(send, SEQ, 3)
        xb[me, span, :] = one_row(start, rows, me)

    loads[0].wait()
    for i in range(1, 9):
        loads[i].start()
    gate_rows(32, 32)
    pl.semaphore_wait(barrier, SEQ + CHAN - 2)
    halo = pltpu.make_async_remote_copy(
        src_ref=streams.at[:, :, pl.ds(SLAB - 128, 128)],
        dst_ref=st.at[:, :, pl.ds(0, 128)],
        send_sem=halo_sem.at[0],
        recv_sem=halo_sem.at[1],
        device_id={"seq": lax.rem(me + 1, SEQ)},
        device_id_type=MESH,
    )
    halo.start()
    send_rows(0, 32, 32)

    def send_more(n, c):
        start = n * 32 + 32
        gate_rows(start, 32)
        send_rows(n, start, 32)
        return c

    lax.fori_loop(1, 3, send_more, 0)
    gate_rows(16, 16)
    send_rows(3, 16, 16)
    halo.wait()
    rim = st[:, :, pl.ds(0, 128)]
    st[:, :, pl.ds(0, 128)] = jnp.where(me > 0, rim, jnp.zeros_like(rim))
    gate_rows(0, 16)
    send_rows(4, 0, 16)

    for i in (1, 2, 3):
        loads[i].wait()
    filter_prep(hv, sh, hs, pick, perm, skip[me] * 2.0**-20)
    loads[4].wait()

    def gate_tiles(i, c):
        first = i * TILES
        vals = short_conv(0, first)
        for k in range(TILES):
            gate[:, pl.ds(pl.multiple_of((first + k) * 128, 128), 128)] = vals[k].astype(BF16)
        return c

    lax.fori_loop(0, 128 // TILES, gate_tiles, 0)
    for i in (5, 6, 7, 8):
        loads[i].wait()

    def all_of(buf, start, rows, sem):
        part = buf.at[pl.ds(0, SEQ - 1), pl.ds(pl.multiple_of(start, 16), rows)]
        return pltpu.make_async_copy(part, part, sem)

    def transform_rows(n, start, rows):
        all_of(xb, start, rows, x_recv.at[n]).wait()

        def part(k, c):
            r = pl.multiple_of(start + k * 16, 16)
            stage_one(lambda s: xb[s, pl.ds(r, 16), :].astype(F32), a, w1, r)
            return c

        lax.fori_loop(0, rows // 16, part, 0)

    def transform_more(n, c):
        transform_rows(n, n * 32 + 32, 32)
        return c

    def transform_last(n, c):
        transform_rows(n, (4 - n) * 16, 16)
        return c

    lax.fori_loop(0, 3, transform_more, 0)
    lax.fori_loop(3, 5, transform_last, 0)
    all_middle(a, g, hs, uv, t0)

    def back_rows(n, start, rows):
        def part(k, c):
            r = pl.multiple_of(start + k * 16, 16)
            ys = stage_last(g, w1, r)
            for s in range(SEQ):
                yb[s, pl.ds(r, 16), :] = ys[s].astype(BF16)
            return c

        lax.fori_loop(0, rows // 16, part, 0)
        span = pl.ds(pl.multiple_of(start, 16), rows)

        def send(i):
            peer = seq_peer(i)
            pltpu.make_async_remote_copy(
                src_ref=yb.at[peer, span],
                dst_ref=rb.at[me, span],
                send_sem=y_send.at[n],
                recv_sem=y_recv.at[n],
                device_id={"seq": peer},
                device_id_type=MESH,
            ).start()

        each_peer(send, SEQ, 5)
        rb[me, span, :] = yb[me, span, :]

    def back_more(n, c):
        back_rows(n, n * 32 - 16, 32)
        return c

    back_rows(0, 0, 16)
    lax.fori_loop(1, 4, back_more, 0)
    back_rows(4, 112, 16)

    def sums_of(start, rows, sem):
        part = sqa.at[pl.ds(0, CHAN - 1), pl.ds(pl.multiple_of(start, 16), rows)]
        return pltpu.make_async_copy(part, part, sem)

    def hidden_out(n, start, rows):
        cols = pl.ds(pl.multiple_of(start * 128, 128), rows * 128)
        return pltpu.make_async_copy(hb.at[:, cols], out_h.at[:, cols], o_sem.at[n])

    def combine(n, start, rows):
        all_of(rb, start, rows, y_recv.at[n]).wait()
        span = pl.ds(pl.multiple_of(start, 16), rows)

        def spread_row(ch, c):
            flat[pl.ds(start * 32 + ch, rows, stride=32), :] = rb[ch, span, :].astype(F32)
            return c

        lax.fori_loop(0, 32, spread_row, 0, unroll=8)

        def tile(r, c):
            p = start + r
            cols = pl.ds(pl.multiple_of(p * 128, 128), 128)
            long_out = flat[pl.ds(pl.multiple_of(p * 32, 32), 32), :]
            hidden = (res[:, cols].astype(F32) + gate[:, cols].astype(F32) * long_out).astype(BF16)
            hb[:, cols] = hidden
            wide = hidden.astype(F32)
            sqp[pl.ds(p, 1), :] = jnp.sum(wide * wide, axis=0, keepdims=True)
            return c

        lax.fori_loop(0, rows, tile, 0, unroll=8)

        def send(i):
            pltpu.make_async_remote_copy(
                src_ref=sqp.at[span],
                dst_ref=sqa.at[mc, span],
                send_sem=s_send.at[n],
                recv_sem=s_recv.at[n],
                device_id={"chan": chan_peer(i)},
                device_id_type=MESH,
            ).start()

        each_peer(send, CHAN, 7)
        sqa[mc, span, :] = sqp[span, :]
        hidden_out(n, start, rows).start()

    def norm(n, start, rows):
        sums_of(start, rows, s_recv.at[n]).wait()
        span = pl.ds(pl.multiple_of(start, 16), rows)
        total = sqa[0, span, :]
        for k in range(1, CHAN):
            total = total + sqa[k, span, :]
        rs[span, :] = lax.rsqrt(total * (1.0 / (32 * CHAN)) + 1e-06)

    def combine_more(n, c):
        combine(n, n * 32 - 16, 32)
        return c

    def norm_more(n, c):
        norm(n, n * 32 - 16, 32)
        return c

    combine(0, 0, 16)
    lax.fori_loop(1, 4, combine_more, 0)
    combine(4, 112, 16)
    norm(0, 0, 16)
    lax.fori_loop(1, 4, norm_more, 0)
    norm(4, 112, 16)
    scale_out = pltpu.make_async_copy(rs, out_r, o_sem.at[5])
    scale_out.start()
    for n, start, rows in THERE:
        all_of(xb, start, rows, x_send.at[n]).wait()
    for n, start, rows in BACK:
        all_of(rb, start, rows, y_send.at[n]).wait()
        sums_of(start, rows, s_send.at[n]).wait()
        hidden_out(n, start, rows).wait()
    scale_out.wait()


PARTS = 4


def finish(hidden, scale, gain, out_h, out_n, hb, nb, rs, gb, in_sem, out_sem):
    size = SLAB // PARTS

    def cols(j):
        return pl.ds(j * size, size)

    scale_in = pltpu.make_async_copy(scale, rs, in_sem.at[PARTS])
    scale_in.start()
    ins = [
        pltpu.make_async_copy(hidden.at[:, cols(j)], hb.at[:, cols(j)], in_sem.at[j])
        for j in range(PARTS)
    ]
    for copy in ins:
        copy.start()
    eye = lax.broadcasted_iota(jnp.int32, (32, 32), 0) == lax.broadcasted_iota(
        jnp.int32, (32, 32), 1
    )
    column = jnp.sum(jnp.where(eye, gain[...], 0.0), axis=1, keepdims=True)
    gb[...] = jnp.broadcast_to(column, (32, 128))
    scale_in.wait()
    outs = []
    for j in range(PARTS):
        ins[j].wait()
        outs.append(pltpu.make_async_copy(hb.at[:, cols(j)], out_h.at[:, cols(j)], out_sem.at[0, j]))
        outs[-1].start()

        def tile(r, c):
            p = j * (128 // PARTS) + r
            here = pl.ds(pl.multiple_of(p * 128, 128), 128)
            nb[:, here] = (hb[:, here].astype(F32) * (gb[...] * rs[pl.ds(p, 1), :])).astype(BF16)
            return c

        lax.fori_loop(0, 128 // PARTS, tile, 0, unroll=8)
        outs.append(pltpu.make_async_copy(nb.at[:, cols(j)], out_n.at[:, cols(j)], out_sem.at[1, j]))
        outs[-1].start()
    for copy in outs:
        copy.wait()


def per_device(streams, conv_weights, skip, filter_spec, residual, gain):
    tables = [jnp.asarray(t) for t in make_tables()]
    h2 = filter_spec.reshape(2, 8192, 128).transpose(1, 0, 2).reshape(16384, 128)
    far = pl.BlockSpec(memory_space=pl.ANY)
    near = pl.BlockSpec(memory_space=pltpu.VMEM)
    slab = (32, SLAB)
    dma = pltpu.SemaphoreType.DMA
    vmem = pltpu.VMEM
    line = gain.reshape(1, 32)
    hidden, scale = pl.pallas_call(
        fused,
        out_shape=[
            jax.ShapeDtypeStruct(slab, BF16),
            jax.ShapeDtypeStruct((128, 128), F32),
        ],
        in_specs=[far, near, pl.BlockSpec(memory_space=pltpu.SMEM), far, far, near] + [far] * 5,
        out_specs=[far, far],
        scratch_shapes=[
            vmem((3, 32, 128 + SLAB), BF16),
            vmem((4096, 128), F32),
            vmem((32, 128, 128), BF16),
            vmem((32, 128, 128), BF16),
            vmem((16384, 128), BF16),
            vmem((SLOTS * 256, 128), F32),
            vmem((ROWS, 2, 128, 128), F32),
            vmem((ROWS, 256, 128), BF16),
            vmem((ROWS, 256, 128), F32),
            vmem((2, 256, 256), BF16),
            vmem((2, 128, 128), F32),
            vmem((ROWS, 2, 128, 128), F32),
            vmem((4 * SLOTS, 128), BF16),
            vmem((512, 256), BF16),
            vmem((32, 128, 128), BF16),
            vmem((32, 128, 128), BF16),
            vmem(slab, BF16),
            vmem(slab, BF16),
            vmem(slab, BF16),
            vmem((128, 128), F32),
            vmem((CHAN, 128, 128), F32),
            vmem((128, 128), F32),
            vmem((9, 32, 128), F32),
            dma((9,)),
            dma((2,)),
            dma((5,)),
            dma((5,)),
            dma((5,)),
            dma((5,)),
            dma((5,)),
            dma((5,)),
            dma((6,)),
        ],
        compiler_params=pltpu.CompilerParams(
            collective_id=0, has_side_effects=True, vmem_limit_bytes=60 * 2**20
        ),
        cost_estimate=pl.CostEstimate(
            flops=8 * 10**9, bytes_accessed=20 * 2**20, transcendentals=0
        ),
    )(streams, conv_weights.transpose(0, 2, 1), skip, h2, residual, line, *tables)
    return pl.pallas_call(
        finish,
        out_shape=[jax.ShapeDtypeStruct(slab, BF16)] * 2,
        in_specs=[far, far, near],
        out_specs=[far, far],
        scratch_shapes=[
            vmem(slab, BF16),
            vmem(slab, BF16),
            vmem((128, 128), F32),
            vmem((32, 128), F32),
            dma((PARTS + 1,)),
            dma((2, PARTS)),
        ],
        compiler_params=pltpu.CompilerParams(vmem_limit_bytes=60 * 2**20),
        cost_estimate=pl.CostEstimate(
            flops=3 * 2**19, bytes_accessed=3 * 2**20, transcendentals=0
        ),
    )(hidden, scale, line)


def solution(mesh):
    in_specs = (
        P(None, "chan", "seq"),
        P(None, "chan", None),
        P("chan"),
        P("chan", "seq", None, None),
        P("chan", "seq"),
        P("chan"),
    )
    return jax.shard_map(
        lambda *args: tuple(per_device(*args)),
        mesh=mesh,
        in_specs=in_specs,
        out_specs=(P("chan", "seq"), P("chan", "seq")),
        check_vma=False,
    )
```

time: 87.5 us -> 78.4 us (0.90)
  Pallas kernels: 82.2 us -> 77.6 us
  local copies, waits for them, and re-layouts: 4.52 us -> 0 us
    pallas_call x1 -> x2, Pallas kernels: 82.2 us -> 77.6 us  [the longest x1 74.5 us: per_device(): pl.pallas_call(fused, out_shape=[jax.ShapeDtypeStruct(slab, BF16), jax.Sh...]
    unnamed x2 -> x0, local copies, waits for them, and re-layouts: 4.52 us -> none
where the time goes in v2:
time: 78.4 us; the launch traced here: 78.2 us
  Pallas kernels  77.6 us (99%)
    pallas_call x1, Pallas kernels, per_device(): pl.pallas_call(fused, out_shape=[jax.ShapeDtypeStruct(slab, BF16), jax.Sh...  74.5 us
    pallas_call x1, Pallas kernels, per_device(): pl.pallas_call(finish, out_shape=[jax.ShapeDtypeStruct(slab, BF16)] * 2,...  3.09 us

profile of v2, /device:TPU:1, one launch (start us, length us, event | category | flops | bytes accessed | tf_op | source)
XLA Modules:
  0.0 78.2 jit_solution(12356708877793212164)
XLA Ops:
  0.6 74.5 %shard_map.122 = (bf16[32,16384]{1,0:T(8,128)(2,1)}, f32[128,128]{1,0:T(8,128)}) custom-call(bf16[3,32,16384]{2,1,0:T(8,128)(2,1)} %streams.1, f32[3,3,32]{2,1,0:T(4,128)} %bitcast.10, f32[32]{0:T(128)} %skip.1, bf16[16384,128]{1,0:T(8,128)(2,1)} %bitcast.9, bf16[32,16384]{1,0:T(8,128)(2,1)} %residual.1, f32[1,32]{1,0:T(1,128)} %bitcast.7, ...), custom_call_target="tpu_custom_call" | custom-call | flops 8000000000 | bytes 20971520 | tf_op jit(solution)/shard_map/pallas_call | solution.py:651
  75.1 3.1 %shard_map.123 = (bf16[32,16384]{1,0:T(8,128)(2,1)}, bf16[32,16384]{1,0:T(8,128)(2,1)}) custom-call(bf16[32,16384]{1,0:T(8,128)(2,1)} %get-tuple-element.4.hidden, f32[128,128]{1,0:T(8,128)} %get-tuple-element.5.scale, f32[1,32]{1,0:T(1,128)} %bitcast.8), custom_call_target="tpu_custom_call" | custom-call | flops 1572864 | bytes 3145728 | tf_op jit(solution)/shard_map/pallas_call | solution.py:700

commit v3 on v2

--- a/solution.py
+++ b/solution.py
@@ -157,7 +157,7 @@
             i += 1
 
 
-def filter_prep(h_ref, sh, hs, pick_ref, perm_ref, direct, unroll=4):
+def filter_prep(h_ref, sh, hs, pick_ref, perm_ref, direct, unroll=8):
     pick = pick_ref[...]
     perm = perm_ref[...]
 
@@ -173,13 +173,26 @@
 
     lax.fori_loop(0, 64 // unroll, step, 0)
 
+    same = (
+        lax.broadcasted_iota(jnp.int32, (128, 128), 0)
+        == lax.broadcasted_iota(jnp.int32, (128, 128), 1)
+    ).astype(BF16)
+
     def turn_over(i, c):
-        for part in range(2):
-            row = pl.multiple_of(i * 256 + part * 128, 128)
-            hs[i, part] = sh[pl.ds(row, 128), :].T
-        return c
-
-    lax.fori_loop(0, ROWS, turn_over, 0)
+        planes = []
+        for j in range(11):
+            row = pl.multiple_of((i * 11 + j) * 256, 256)
+            planes.append(sh[pl.ds(row, 256), :].astype(BF16))
+        turned = [
+            lax.dot_general(same, x, (((1,), (1,)), ((), ())), preferred_element_type=F32)
+            for x in planes
+        ]
+        for j in range(11):
+            for part in range(2):
+                hs[i * 11 + j, part] = turned[j][:, part * 128 : (part + 1) * 128]
+        return c
+
+    lax.fori_loop(0, ROWS // 11, turn_over, 0)
 
 
 def stage_one(load, a_ref, w1_ref, row, height=16):
@@ -291,8 +304,9 @@
 SLAB = 16384
 TILES = 4
 MESH = pl.DeviceIdType.MESH
-THERE = [(0, 32, 32), (1, 64, 32), (2, 96, 32), (3, 16, 16), (4, 0, 16)]
+THERE = [(0, 112, 16), (1, 80, 32), (2, 48, 32), (3, 16, 32), (4, 0, 16)]
 BACK = [(0, 0, 16), (1, 16, 32), (2, 48, 32), (3, 80, 32), (4, 112, 16)]
+EARLY = 2
 
 
 def each_peer(fn, count, per):
@@ -308,11 +322,11 @@
 
 
 def fused(
-    streams, wts, skip, h2, residual, gain, uv_in, t0_in, w1_in, pick_in, perm_in,
+    streams, wts, skip, h2, residual, uv_in, t0_in, w1_in, pick_in, perm_in,
     out_h, out_r,
     st, flat, sb, xb, hv, sh, hs, a, g, uv, t0, w1, pick, perm, yb, rb,
     gate, res, hb, sqp, sqa, rs, wb,
-    load_sem, halo_sem, x_send, x_recv, y_send, y_recv, s_send, s_recv, o_sem,
+    piece_sem, load_sem, halo_sem, x_send, x_recv, y_send, y_recv, s_send, s_recv, o_sem,
 ):
     me = lax.axis_index("seq")
     mc = lax.axis_index("chan")
@@ -323,22 +337,34 @@
     def chan_peer(i):
         return lax.rem(mc + i, CHAN)
 
+    def stream_piece(n, first, tiles):
+        here = pl.ds(first * 128, tiles * 128)
+        there = pl.ds(first * 128 + 128, tiles * 128)
+        return pltpu.make_async_copy(
+            streams.at[pl.ds(1, 2), :, here], st.at[pl.ds(1, 2), :, there], piece_sem.at[n]
+        )
+
+    pieces = [
+        stream_piece(0, 111, 17),
+        stream_piece(1, 79, 32),
+        stream_piece(2, 47, 32),
+        stream_piece(3, 15, 32),
+        stream_piece(4, 0, 15),
+    ]
     loads = [
+        pltpu.make_async_copy(h2, hv, load_sem.at[0]),
+        pltpu.make_async_copy(pick_in, pick, load_sem.at[1]),
+        pltpu.make_async_copy(perm_in, perm, load_sem.at[2]),
         pltpu.make_async_copy(
-            streams.at[pl.ds(1, 2)], st.at[pl.ds(1, 2), :, pl.ds(128, SLAB)], load_sem.at[0]
+            streams.at[pl.ds(0, 1)], st.at[pl.ds(0, 1), :, pl.ds(128, SLAB)], load_sem.at[3]
         ),
-        pltpu.make_async_copy(h2, hv, load_sem.at[1]),
-        pltpu.make_async_copy(pick_in, pick, load_sem.at[2]),
-        pltpu.make_async_copy(perm_in, perm, load_sem.at[3]),
-        pltpu.make_async_copy(
-            streams.at[pl.ds(0, 1)], st.at[pl.ds(0, 1), :, pl.ds(128, SLAB)], load_sem.at[4]
-        ),
-        pltpu.make_async_copy(w1_in, w1, load_sem.at[5]),
-        pltpu.make_async_copy(uv_in, uv, load_sem.at[6]),
-        pltpu.make_async_copy(t0_in, t0, load_sem.at[7]),
-        pltpu.make_async_copy(residual, res, load_sem.at[8]),
+        pltpu.make_async_copy(w1_in, w1, load_sem.at[4]),
+        pltpu.make_async_copy(uv_in, uv, load_sem.at[5]),
+        pltpu.make_async_copy(t0_in, t0, load_sem.at[6]),
+        pltpu.make_async_copy(residual, res, load_sem.at[7]),
     ]
-    loads[0].start()
+    for copy in pieces:
+        copy.start()
 
     barrier = pltpu.get_barrier_semaphore()
 
@@ -396,28 +422,44 @@
     def one_row(start, rows, c):
         return flat[pl.ds(start * 32 + c, rows, stride=32), :].astype(BF16)
 
-    def send_rows(n, start, rows):
+    def prepare(start, rows):
         span = pl.ds(pl.multiple_of(start, 16), rows)
 
+        def take(c):
+            sb[c, span, :] = one_row(start, rows, c)
+
+        def step(i, c):
+            for k in range(4):
+                take(i * 4 + k)
+            return c
+
+        lax.fori_loop(0, 8, step, 0)
+        xb[me, span, :] = sb[me, span, :]
+
+    def send_to(peer, n, start, rows):
+        span = pl.ds(pl.multiple_of(start, 16), rows)
+        pltpu.make_async_remote_copy(
+            src_ref=sb.at[peer, span],
+            dst_ref=xb.at[me, span],
+            send_sem=x_send.at[n],
+            recv_sem=x_recv.at[n],
+            device_id={"seq": peer},
+            device_id_type=MESH,
+        ).start()
+
+    def send_rows(core, n, start, rows):
         def send(i):
-            peer = seq_peer(i)
-            sb[peer, span, :] = one_row(start, rows, peer)
-            pltpu.make_async_remote_copy(
-                src_ref=sb.at[peer, span],
-                dst_ref=xb.at[me, span],
-                send_sem=x_send.at[n],
-                recv_sem=x_recv.at[n],
-                device_id={"seq": peer},
-                device_id_type=MESH,
-            ).start()
-
-        each_peer(send, SEQ, 3)
-        xb[me, span, :] = one_row(start, rows, me)
-
-    loads[0].wait()
-    for i in range(1, 9):
-        loads[i].start()
-    gate_rows(32, 32)
+            send_to(lax.rem(me // 2 + i * 5, SEQ // 2) * 2 + core, n, start, rows)
+
+        each_peer(send, SEQ // 2, 5)
+
+    def first_sends(n, start, rows):
+        prepare(start, rows)
+        send_rows(0, n, start, rows)
+        send_to(me + 1 - 2 * lax.rem(me, 2), n, start, rows)
+
+    pieces[0].wait()
+    gate_rows(112, 16)
     pl.semaphore_wait(barrier, SEQ + CHAN - 2)
     halo = pltpu.make_async_remote_copy(
         src_ref=streams.at[:, :, pl.ds(SLAB - 128, 128)],
@@ -428,37 +470,37 @@
         device_id_type=MESH,
     )
     halo.start()
-    send_rows(0, 32, 32)
+    first_sends(0, 112, 16)
+    for i in range(1, 5):
+        pieces[i].wait()
+    for copy in loads:
+        copy.start()
 
     def send_more(n, c):
-        start = n * 32 + 32
+        start = 112 - n * 32
         gate_rows(start, 32)
-        send_rows(n, start, 32)
-        return c
-
-    lax.fori_loop(1, 3, send_more, 0)
-    gate_rows(16, 16)
-    send_rows(3, 16, 16)
+        first_sends(n, start, 32)
+        return c
+
+    lax.fori_loop(1, 4, send_more, 0)
     halo.wait()
     rim = st[:, :, pl.ds(0, 128)]
     st[:, :, pl.ds(0, 128)] = jnp.where(me > 0, rim, jnp.zeros_like(rim))
     gate_rows(0, 16)
-    send_rows(4, 0, 16)
-
-    for i in (1, 2, 3):
+    first_sends(4, 0, 16)
+
+    def second_sends(n, c):
+        send_rows(1, n, 112 - n * 32, 32)
+        return c
+
+    send_rows(1, 0, 112, 16)
+    lax.fori_loop(1, 4, second_sends, 0)
+    send_rows(1, 4, 0, 16)
+
+    for i in (0, 1, 2):
         loads[i].wait()
     filter_prep(hv, sh, hs, pick, perm, skip[me] * 2.0**-20)
-    loads[4].wait()
-
-    def gate_tiles(i, c):
-        first = i * TILES
-        vals = short_conv(0, first)
-        for k in range(TILES):
-            gate[:, pl.ds(pl.multiple_of((first + k) * 128, 128), 128)] = vals[k].astype(BF16)
-        return c
-
-    lax.fori_loop(0, 128 // TILES, gate_tiles, 0)
-    for i in (5, 6, 7, 8):
+    for i in (4, 5, 6):
         loads[i].wait()
 
     def all_of(buf, start, rows, sem):
@@ -476,18 +518,15 @@
         lax.fori_loop(0, rows // 16, part, 0)
 
     def transform_more(n, c):
-        transform_rows(n, n * 32 + 32, 32)
-        return c
-
-    def transform_last(n, c):
-        transform_rows(n, (4 - n) * 16, 16)
-        return c
-
-    lax.fori_loop(0, 3, transform_more, 0)
-    lax.fori_loop(3, 5, transform_last, 0)
+        transform_rows(n, 112 - n * 32, 32)
+        return c
+
+    transform_rows(0, 112, 16)
+    lax.fori_loop(1, 4, transform_more, 0)
+    transform_rows(4, 0, 16)
     all_middle(a, g, hs, uv, t0)
 
-    def back_rows(n, start, rows):
+    def back_rows(start, rows):
         def part(k, c):
             r = pl.multiple_of(start + k * 16, 16)
             ys = stage_last(g, w1, r)
@@ -497,29 +536,65 @@
 
         lax.fori_loop(0, rows // 16, part, 0)
         span = pl.ds(pl.multiple_of(start, 16), rows)
-
+        rb[me, span, :] = yb[me, span, :]
+
+    def send_back(peer, n, start, rows):
+        span = pl.ds(pl.multiple_of(start, 16), rows)
+        pltpu.make_async_remote_copy(
+            src_ref=yb.at[peer, span],
+            dst_ref=rb.at[me, span],
+            send_sem=y_send.at[n],
+            recv_sem=y_recv.at[n],
+            device_id={"seq": peer},
+            device_id_type=MESH,
+        ).start()
+
+    def back_more(n, c):
+        start = n * 32 - 16
+        back_rows(start, 32)
+        each_peer(lambda i: send_back(seq_peer(i), n, start, 32), SEQ, 5)
+        return c
+
+    def z_of(peer):
+        return lax.rem(peer // 2, 8)
+
+    def to_early(i):
+        peer = seq_peer(i)
+
+        @pl.when(z_of(peer) < EARLY)
+        def _():
+            send_back(peer, *BACK[3])
+            send_back(peer, *BACK[4])
+
+    def to_late(chunk):
         def send(i):
             peer = seq_peer(i)
-            pltpu.make_async_remote_copy(
-                src_ref=yb.at[peer, span],
-                dst_ref=rb.at[me, span],
-                send_sem=y_send.at[n],
-                recv_sem=y_recv.at[n],
-                device_id={"seq": peer},
-                device_id_type=MESH,
-            ).start()
-
-        each_peer(send, SEQ, 5)
-        rb[me, span, :] = yb[me, span, :]
-
-    def back_more(n, c):
-        back_rows(n, n * 32 - 16, 32)
-        return c
-
-    back_rows(0, 0, 16)
-    lax.fori_loop(1, 4, back_more, 0)
-    back_rows(4, 112, 16)
-
+
+            @pl.when(z_of(peer) >= EARLY)
+            def _():
+                send_back(peer, *chunk)
+
+        return send
+
+    back_rows(0, 16)
+    each_peer(lambda i: send_back(seq_peer(i), *BACK[0]), SEQ, 5)
+    lax.fori_loop(1, 3, back_more, 0)
+    back_rows(80, 48)
+    each_peer(to_early, SEQ, 5)
+    each_peer(to_late(BACK[3]), SEQ, 5)
+    each_peer(to_late(BACK[4]), SEQ, 5)
+
+    for i in (3, 7):
+        loads[i].wait()
+
+    def gate_tiles(i, c):
+        first = i * TILES
+        vals = short_conv(0, first)
+        for k in range(TILES):
+            gate[:, pl.ds(pl.multiple_of((first + k) * 128, 128), 128)] = vals[k].astype(BF16)
+        return c
+
+    lax.fori_loop(0, 128 // TILES, gate_tiles, 0)
     def sums_of(start, rows, sem):
         part = sqa.at[pl.ds(0, CHAN - 1), pl.ds(pl.multiple_of(start, 16), rows)]
         return pltpu.make_async_copy(part, part, sem)
@@ -654,7 +729,7 @@
             jax.ShapeDtypeStruct(slab, BF16),
             jax.ShapeDtypeStruct((128, 128), F32),
         ],
-        in_specs=[far, near, pl.BlockSpec(memory_space=pltpu.SMEM), far, far, near] + [far] * 5,
+        in_specs=[far, near, pl.BlockSpec(memory_space=pltpu.SMEM)] + [far] * 7,
         out_specs=[far, far],
         scratch_shapes=[
             vmem((3, 32, 128 + SLAB), BF16),
@@ -680,7 +755,8 @@
             vmem((CHAN, 128, 128), F32),
             vmem((128, 128), F32),
             vmem((9, 32, 128), F32),
-            dma((9,)),
+            dma((5,)),
+            dma((8,)),
             dma((2,)),
             dma((5,)),
             dma((5,)),
@@ -696,7 +772,7 @@
         cost_estimate=pl.CostEstimate(
             flops=8 * 10**9, bytes_accessed=20 * 2**20, transcendentals=0
         ),
-    )(streams, conv_weights.transpose(0, 2, 1), skip, h2, residual, line, *tables)
+    )(streams, conv_weights.transpose(0, 2, 1), skip, h2, residual, *tables)
     return pl.pallas_call(
         finish,
         out_shape=[jax.ShapeDtypeStruct(slab, BF16)] * 2,

time: 78.4 us -> 70 us (0.89)
  Pallas kernels: 77.6 us -> 69.2 us
    pallas_call x1, Pallas kernels: 74.5 us -> 66.1 us  [per_device(): pl.pallas_call(fused, out_shape=[jax.ShapeDtypeStruct(slab, BF16), jax.Sh...]
where the time goes in v3:
time: 70 us; the launch traced here: 69.8 us
  Pallas kernels  69.2 us (99%)
    pallas_call x1, Pallas kernels, per_device(): pl.pallas_call(fused, out_shape=[jax.ShapeDtypeStruct(slab, BF16), jax.Sh...  66.1 us
    pallas_call x1, Pallas kernels, per_device(): pl.pallas_call(finish, out_shape=[jax.ShapeDtypeStruct(slab, BF16)] * 2,...  3.09 us

profile of v3, /device:TPU:1, one launch (start us, length us, event | category | flops | bytes accessed | tf_op | source)
XLA Modules:
  0.0 69.8 jit_solution(10688487675879452659)
XLA Ops:
  0.6 66.1 %shard_map.122 = (bf16[32,16384]{1,0:T(8,128)(2,1)}, f32[128,128]{1,0:T(8,128)}) custom-call(bf16[3,32,16384]{2,1,0:T(8,128)(2,1)} %streams.1, f32[3,3,32]{2,1,0:T(4,128)} %bitcast.9, f32[32]{0:T(128)} %skip.1, bf16[16384,128]{1,0:T(8,128)(2,1)} %bitcast.8, bf16[32,16384]{1,0:T(8,128)(2,1)} %residual.1, bf16[2,256,256]{2,1,0:T(8,128)(2,1)} %constant.10.clone.uv_in, ...), custom_call_target="tpu_custom_call" | custom-call | flops 8000000000 | bytes 20971520 | tf_op jit(solution)/shard_map/pallas_call | solution.py:726
  66.7 3.1 %shard_map.123 = (bf16[32,16384]{1,0:T(8,128)(2,1)}, bf16[32,16384]{1,0:T(8,128)(2,1)}) custom-call(bf16[32,16384]{1,0:T(8,128)(2,1)} %get-tuple-element.4.hidden, f32[128,128]{1,0:T(8,128)} %get-tuple-element.5.scale, f32[1,32]{1,0:T(1,128)} %bitcast.7), custom_call_target="tpu_custom_call" | custom-call | flops 1572864 | bytes 3145728 | tf_op jit(solution)/shard_map/pallas_call | solution.py:776

commit v4 on v3

--- a/solution.py
+++ b/solution.py
@@ -306,7 +306,7 @@
 MESH = pl.DeviceIdType.MESH
 THERE = [(0, 112, 16), (1, 80, 32), (2, 48, 32), (3, 16, 32), (4, 0, 16)]
 BACK = [(0, 0, 16), (1, 16, 32), (2, 48, 32), (3, 80, 32), (4, 112, 16)]
-EARLY = 2
+LAST = [(0, 1, 3), (0, 1, 4), (1, 3, 3), (1, 3, 4), (3, 8, 3), (3, 8, 4)]
 
 
 def each_peer(fn, count, per):
@@ -322,11 +322,11 @@
 
 
 def fused(
-    streams, wts, skip, h2, residual, uv_in, t0_in, w1_in, pick_in, perm_in,
-    out_h, out_r,
+    streams, wts, skip, h2, residual, gain, uv_in, t0_in, w1_in, pick_in, perm_in,
+    hb, nb,
     st, flat, sb, xb, hv, sh, hs, a, g, uv, t0, w1, pick, perm, yb, rb,
-    gate, res, hb, sqp, sqa, rs, wb,
-    piece_sem, load_sem, halo_sem, x_send, x_recv, y_send, y_recv, s_send, s_recv, o_sem,
+    gate, res, sqp, sqa, rs, wb,
+    piece_sem, load_sem, halo_sem, x_send, x_recv, y_send, y_recv, s_send, s_recv,
 ):
     me = lax.axis_index("seq")
     mc = lax.axis_index("chan")
@@ -390,6 +390,7 @@
     for stream in range(3):
         for tap in range(3):
             wb[stream * 3 + tap] = spread(wts[stream, pl.ds(tap, 1), :])
+    wb[9] = spread(gain[...])
 
     lane = lax.broadcasted_iota(jnp.int32, (32, 128), 1)
 
@@ -558,19 +559,11 @@
     def z_of(peer):
         return lax.rem(peer // 2, 8)
 
-    def to_early(i):
-        peer = seq_peer(i)
-
-        @pl.when(z_of(peer) < EARLY)
-        def _():
-            send_back(peer, *BACK[3])
-            send_back(peer, *BACK[4])
-
-    def to_late(chunk):
+    def to_planes(low, high, chunk):
         def send(i):
             peer = seq_peer(i)
 
-            @pl.when(z_of(peer) >= EARLY)
+            @pl.when((z_of(peer) >= low) & (z_of(peer) < high))
             def _():
                 send_back(peer, *chunk)
 
@@ -580,9 +573,8 @@
     each_peer(lambda i: send_back(seq_peer(i), *BACK[0]), SEQ, 5)
     lax.fori_loop(1, 3, back_more, 0)
     back_rows(80, 48)
-    each_peer(to_early, SEQ, 5)
-    each_peer(to_late(BACK[3]), SEQ, 5)
-    each_peer(to_late(BACK[4]), SEQ, 5)
+    for low, high, n in LAST:
+        each_peer(to_planes(low, high, BACK[n]), SEQ, 5)
 
     for i in (3, 7):
         loads[i].wait()
@@ -598,10 +590,6 @@
     def sums_of(start, rows, sem):
         part = sqa.at[pl.ds(0, CHAN - 1), pl.ds(pl.multiple_of(start, 16), rows)]
         return pltpu.make_async_copy(part, part, sem)
-
-    def hidden_out(n, start, rows):
-        cols = pl.ds(pl.multiple_of(start * 128, 128), rows * 128)
-        return pltpu.make_async_copy(hb.at[:, cols], out_h.at[:, cols], o_sem.at[n])
 
     def combine(n, start, rows):
         all_of(rb, start, rows, y_recv.at[n]).wait()
@@ -637,7 +625,6 @@
 
         each_peer(send, CHAN, 7)
         sqa[mc, span, :] = sqp[span, :]
-        hidden_out(n, start, rows).start()
 
     def norm(n, start, rows):
         sums_of(start, rows, s_recv.at[n]).wait()
@@ -647,6 +634,14 @@
             total = total + sqa[k, span, :]
         rs[span, :] = lax.rsqrt(total * (1.0 / (32 * CHAN)) + 1e-06)
 
+        def tile(r, c):
+            p = start + r
+            cols = pl.ds(pl.multiple_of(p * 128, 128), 128)
+            nb[:, cols] = (hb[:, cols].astype(F32) * (wb[9] * rs[pl.ds(p, 1), :])).astype(BF16)
+            return c
+
+        lax.fori_loop(0, rows, tile, 0, unroll=8)
+
     def combine_more(n, c):
         combine(n, n * 32 - 16, 32)
         return c
@@ -661,56 +656,25 @@
     norm(0, 0, 16)
     lax.fori_loop(1, 4, norm_more, 0)
     norm(4, 112, 16)
-    scale_out = pltpu.make_async_copy(rs, out_r, o_sem.at[5])
-    scale_out.start()
     for n, start, rows in THERE:
         all_of(xb, start, rows, x_send.at[n]).wait()
     for n, start, rows in BACK:
         all_of(rb, start, rows, y_send.at[n]).wait()
         sums_of(start, rows, s_send.at[n]).wait()
-        hidden_out(n, start, rows).wait()
-    scale_out.wait()
 
 
 PARTS = 4
 
 
-def finish(hidden, scale, gain, out_h, out_n, hb, nb, rs, gb, in_sem, out_sem):
-    size = SLAB // PARTS
-
-    def cols(j):
-        return pl.ds(j * size, size)
-
-    scale_in = pltpu.make_async_copy(scale, rs, in_sem.at[PARTS])
-    scale_in.start()
-    ins = [
-        pltpu.make_async_copy(hidden.at[:, cols(j)], hb.at[:, cols(j)], in_sem.at[j])
-        for j in range(PARTS)
-    ]
-    for copy in ins:
+def finish(hb, nb, out_h, out_n, out_sem):
+    copies = []
+    for j in range(PARTS):
+        cols = pl.ds(j * (SLAB // PARTS), SLAB // PARTS)
+        copies.append(pltpu.make_async_copy(hb.at[:, cols], out_h.at[:, cols], out_sem.at[0, j]))
+        copies.append(pltpu.make_async_copy(nb.at[:, cols], out_n.at[:, cols], out_sem.at[1, j]))
+    for copy in copies:
         copy.start()
-    eye = lax.broadcasted_iota(jnp.int32, (32, 32), 0) == lax.broadcasted_iota(
-        jnp.int32, (32, 32), 1
-    )
-    column = jnp.sum(jnp.where(eye, gain[...], 0.0), axis=1, keepdims=True)
-    gb[...] = jnp.broadcast_to(column, (32, 128))
-    scale_in.wait()
-    outs = []
-    for j in range(PARTS):
-        ins[j].wait()
-        outs.append(pltpu.make_async_copy(hb.at[:, cols(j)], out_h.at[:, cols(j)], out_sem.at[0, j]))
-        outs[-1].start()
-
-        def tile(r, c):
-            p = j * (128 // PARTS) + r
-            here = pl.ds(pl.multiple_of(p * 128, 128), 128)
-            nb[:, here] = (hb[:, here].astype(F32) * (gb[...] * rs[pl.ds(p, 1), :])).astype(BF16)
-            return c
-
-        lax.fori_loop(0, 128 // PARTS, tile, 0, unroll=8)
-        outs.append(pltpu.make_async_copy(nb.at[:, cols(j)], out_n.at[:, cols(j)], out_sem.at[1, j]))
-        outs[-1].start()
-    for copy in outs:
+    for copy in copies:
         copy.wait()
 
 
@@ -722,15 +686,11 @@
     slab = (32, SLAB)
     dma = pltpu.SemaphoreType.DMA
     vmem = pltpu.VMEM
-    line = gain.reshape(1, 32)
-    hidden, scale = pl.pallas_call(
+    hidden, normed = pl.pallas_call(
         fused,
-        out_shape=[
-            jax.ShapeDtypeStruct(slab, BF16),
-            jax.ShapeDtypeStruct((128, 128), F32),
-        ],
-        in_specs=[far, near, pl.BlockSpec(memory_space=pltpu.SMEM)] + [far] * 7,
-        out_specs=[far, far],
+        out_shape=[vmem(slab, BF16)] * 2,
+        in_specs=[far, near, pl.BlockSpec(memory_space=pltpu.SMEM), far, far, near] + [far] * 5,
+        out_specs=[near, near],
         scratch_shapes=[
             vmem((3, 32, 128 + SLAB), BF16),
             vmem((4096, 128), F32),
@@ -750,11 +710,10 @@
             vmem((32, 128, 128), BF16),
             vmem(slab, BF16),
             vmem(slab, BF16),
-            vmem(slab, BF16),
             vmem((128, 128), F32),
             vmem((CHAN, 128, 128), F32),
             vmem((128, 128), F32),
-            vmem((9, 32, 128), F32),
+            vmem((10, 32, 128), F32),
             dma((5,)),
             dma((8,)),
             dma((2,)),
@@ -764,7 +723,6 @@
             dma((5,)),
             dma((5,)),
             dma((5,)),
-            dma((6,)),
         ],
         compiler_params=pltpu.CompilerParams(
             collective_id=0, has_side_effects=True, vmem_limit_bytes=60 * 2**20
@@ -772,25 +730,20 @@
         cost_estimate=pl.CostEstimate(
             flops=8 * 10**9, bytes_accessed=20 * 2**20, transcendentals=0
         ),
-    )(streams, conv_weights.transpose(0, 2, 1), skip, h2, residual, *tables)
+    )(streams, conv_weights.transpose(0, 2, 1), skip, h2, residual, gain.reshape(1, 32), *tables)
     return pl.pallas_call(
         finish,
         out_shape=[jax.ShapeDtypeStruct(slab, BF16)] * 2,
-        in_specs=[far, far, near],
+        in_specs=[near, near],
         out_specs=[far, far],
         scratch_shapes=[
-            vmem(slab, BF16),
-            vmem(slab, BF16),
-            vmem((128, 128), F32),
-            vmem((32, 128), F32),
-            dma((PARTS + 1,)),
             dma((2, PARTS)),
         ],
-        compiler_params=pltpu.CompilerParams(vmem_limit_bytes=60 * 2**20),
+        compiler_params=pltpu.CompilerParams(vmem_limit_bytes=32 * 2**20),
         cost_estimate=pl.CostEstimate(
-            flops=3 * 2**19, bytes_accessed=3 * 2**20, transcendentals=0
+            flops=0, bytes_accessed=4 * 2**20, transcendentals=0
         ),
-    )(hidden, scale, line)
+    )(hidden, normed)
 
 
 def solution(mesh):

time: 70 us -> 66.9 us (0.956)
  Pallas kernels: 69.2 us -> 66 us
    pallas_call x1, Pallas kernels: 3.09 us -> 1.38 us  [per_device(): pl.pallas_call(finish, out_shape=[jax.ShapeDtypeStruct(slab, BF16)] * 2,...]
    pallas_call x1, Pallas kernels: 66.1 us -> 64.6 us  [per_device(): pl.pallas_call(fused, out_shape=[vmem(slab, BF16)] * 2, in_specs=[far, ne...]
where the time goes in v4:
time: 66.9 us; the launch traced here: 66.6 us
  Pallas kernels  66 us (99%)
    pallas_call x1, Pallas kernels, per_device(): pl.pallas_call(fused, out_shape=[vmem(slab, BF16)] * 2, in_specs=[far, ne...  64.6 us
    pallas_call x1, Pallas kernels, per_device(): pl.pallas_call(finish, out_shape=[jax.ShapeDtypeStruct(slab, BF16)] * 2,...  1.38 us

profile of v4, /device:TPU:1, one launch (start us, length us, event | category | flops | bytes accessed | tf_op | source)
XLA Modules:
  0.0 66.6 jit_solution(4151063142562822215)
XLA Ops:
  0.6 64.6 %shard_map.122 = (bf16[32,16384]{1,0:T(8,128)(2,1)S(1)}, bf16[32,16384]{1,0:T(8,128)(2,1)S(1)}) custom-call(bf16[3,32,16384]{2,1,0:T(8,128)(2,1)} %streams.1, f32[3,3,32]{2,1,0:T(4,128)} %bitcast.8, f32[32]{0:T(128)} %skip.1, bf16[16384,128]{1,0:T(8,128)(2,1)} %bitcast.7, bf16[32,16384]{1,0:T(8,128)(2,1)} %residual.1, f32[1,32]{1,0:T(1,128)} %bitcast.9, ...), custom_call_target="tpu_custom_call" | custom-call | flops 8000000000 | bytes 20971520 | tf_op jit(solution)/shard_map/pallas_call | solution.py:689
  65.3 1.4 %shard_map.123 = (bf16[32,16384]{1,0:T(8,128)(2,1)}, bf16[32,16384]{1,0:T(8,128)(2,1)}) custom-call(bf16[32,16384]{1,0:T(8,128)(2,1)S(1)} %get-tuple-element.4.hb, bf16[32,16384]{1,0:T(8,128)(2,1)S(1)} %get-tuple-element.5.nb), custom_call_target="tpu_custom_call" | custom-call | bytes 4194304 | tf_op jit(solution)/shard_map/pallas_call | solution.py:734

commit v5 on v4

--- a/solution.py
+++ b/solution.py
@@ -302,7 +302,7 @@
 SEQ = 32
 CHAN = 8
 SLAB = 16384
-TILES = 4
+TILES = 8
 MESH = pl.DeviceIdType.MESH
 THERE = [(0, 112, 16), (1, 80, 32), (2, 48, 32), (3, 16, 32), (4, 0, 16)]
 BACK = [(0, 0, 16), (1, 16, 32), (2, 48, 32), (3, 80, 32), (4, 112, 16)]
@@ -363,8 +363,7 @@
         pltpu.make_async_copy(t0_in, t0, load_sem.at[6]),
         pltpu.make_async_copy(residual, res, load_sem.at[7]),
     ]
-    for copy in pieces:
-        copy.start()
+    pieces[0].start()
 
     barrier = pltpu.get_barrier_semaphore()
 
@@ -378,6 +377,8 @@
 
     each_peer(greet_seq, SEQ, 5)
     each_peer(greet_chan, CHAN, 7)
+    for copy in pieces[1:]:
+        copy.start()
 
     eye = lax.broadcasted_iota(jnp.int32, (32, 32), 0) == lax.broadcasted_iota(
         jnp.int32, (32, 32), 1
@@ -455,13 +456,14 @@
         each_peer(send, SEQ // 2, 5)
 
     def first_sends(n, start, rows):
-        prepare(start, rows)
         send_rows(0, n, start, rows)
         send_to(me + 1 - 2 * lax.rem(me, 2), n, start, rows)
 
     pieces[0].wait()
     gate_rows(112, 16)
+    prepare(112, 16)
     pl.semaphore_wait(barrier, SEQ + CHAN - 2)
+    first_sends(0, 112, 16)
     halo = pltpu.make_async_remote_copy(
         src_ref=streams.at[:, :, pl.ds(SLAB - 128, 128)],
         dst_ref=st.at[:, :, pl.ds(0, 128)],
@@ -471,7 +473,6 @@
         device_id_type=MESH,
     )
     halo.start()
-    first_sends(0, 112, 16)
     for i in range(1, 5):
         pieces[i].wait()
     for copy in loads:
@@ -480,6 +481,7 @@
     def send_more(n, c):
         start = 112 - n * 32
         gate_rows(start, 32)
+        prepare(start, 32)
         first_sends(n, start, 32)
         return c
 
@@ -488,6 +490,7 @@
     rim = st[:, :, pl.ds(0, 128)]
     st[:, :, pl.ds(0, 128)] = jnp.where(me > 0, rim, jnp.zeros_like(rim))
     gate_rows(0, 16)
+    prepare(0, 16)
     first_sends(4, 0, 16)
 
     def second_sends(n, c):

time: 66.9 us -> 67 us (level)
  no operation moved by 1% of the time
where the time goes in v5:
time: 67 us; the launch traced here: 66.8 us
  Pallas kernels  66.2 us (99%)
    pallas_call x1, Pallas kernels, per_device(): pl.pallas_call(fused, out_shape=[vmem(slab, BF16)] * 2, in_specs=[far, ne...  64.8 us
    pallas_call x1, Pallas kernels, per_device(): pl.pallas_call(finish, out_shape=[jax.ShapeDtypeStruct(slab, BF16)] * 2,...  1.38 us

profile of v5, /device:TPU:1, one launch (start us, length us, event | category | flops | bytes accessed | tf_op | source)
XLA Modules:
  0.0 66.8 jit_solution(17560926712978508905)
XLA Ops:
  0.6 64.8 %shard_map.122 = (bf16[32,16384]{1,0:T(8,128)(2,1)S(1)}, bf16[32,16384]{1,0:T(8,128)(2,1)S(1)}) custom-call(bf16[3,32,16384]{2,1,0:T(8,128)(2,1)} %streams.1, f32[3,3,32]{2,1,0:T(4,128)} %bitcast.8, f32[32]{0:T(128)} %skip.1, bf16[16384,128]{1,0:T(8,128)(2,1)} %bitcast.7, bf16[32,16384]{1,0:T(8,128)(2,1)} %residual.1, f32[1,32]{1,0:T(1,128)} %bitcast.9, ...), custom_call_target="tpu_custom_call" | custom-call | flops 8000000000 | bytes 20971520 | tf_op jit(solution)/shard_map/pallas_call | solution.py:692
  65.4 1.4 %shard_map.123 = (bf16[32,16384]{1,0:T(8,128)(2,1)}, bf16[32,16384]{1,0:T(8,128)(2,1)}) custom-call(bf16[32,16384]{1,0:T(8,128)(2,1)S(1)} %get-tuple-element.4.hb, bf16[32,16384]{1,0:T(8,128)(2,1)S(1)} %get-tuple-element.5.nb), custom_call_target="tpu_custom_call" | custom-call | bytes 4194304 | tf_op jit(solution)/shard_map/pallas_call | solution.py:737
